TPU v7x, 32 devices: a whole 2x2x4 slice. The times are simulated.
32 devices in a mesh: expert: 8 (over z, y), tensor: 4 (over x, core).
Axes of the slice: x: 2, y: 2, z: 4, core: 2. Of those that a mesh axis runs over, the one named last changes fastest.
Arguments:
- tokens: bfloat16 [2048, 2560], P('expert', 'tensor'), may hold values from -6 to 6
- route_logit: float32 [2048], P('expert'), may hold values from -6 to 6
- expert_ids: int32 [2048, 1], P('expert'), may hold values from 0 to 7; in each aligned block of 256 rows (0 to 255, 256 to 511, ...) at most 40 rows name the same one
- w_gate: bfloat16 [8, 2560, 4096], P('expert', None, 'tensor'), may hold values from -0.125 to 0.125
- w_up: bfloat16 [8, 2560, 4096], P('expert', None, 'tensor'), may hold values from -0.125 to 0.125
- w_down: bfloat16 [8, 4096, 2560], P('expert', 'tensor'), may hold values from -0.09375 to 0.09375
Outputs:
- mixed: bfloat16 [2048, 2560], P('expert', 'tensor')
Inputs may be any that keep to these rules, and one draw needn't show every extreme that they name: `expert_ids`: in each aligned block of 256 tokens no expert id appears more than 40 times, and in some block one expert appears exactly 40 times.
All inputs are finite; a program needn't handle non-finite values.
Results may differ from a plain program's by a relative error of at most 0.0065.
Values may be sent and summed in bfloat16 or wider, within the bound.
A program may use at most 64 MiB of HBM per device.

v0:
```python
import jax
import jax.numpy as jnp
from jax import lax
from jax.sharding import PartitionSpec as P


def on_device(tokens, route_logit, expert_ids, w_gate, w_up, w_down):
    expert_count = lax.axis_size("expert")
    tok_rows, width_local = tokens.shape
    capacity = 5 * tok_rows // (4 * expert_count)
    slot_count = expert_count * capacity
    route = expert_ids[:, 0]
    one_hot = (route[:, None] == jnp.arange(expert_count, dtype=jnp.int32)[None, :]).astype(
        jnp.int32
    )
    earlier = jnp.cumsum(one_hot, axis=0) - one_hot
    position = jnp.sum(earlier * one_hot, axis=1)
    destination = route * capacity + position
    dispatch_map = (
        jnp.arange(slot_count, dtype=jnp.int32)[:, None] == destination[None, :]
    ).astype(jnp.bfloat16)
    factor = jax.nn.sigmoid(route_logit)
    scaled = (factor[:, None] * tokens.astype(jnp.float32)).astype(jnp.bfloat16)
    outgoing = jnp.dot(dispatch_map, scaled, preferred_element_type=jnp.float32).astype(
        jnp.bfloat16
    )
    outgoing = outgoing.reshape(expert_count, capacity, width_local)
    arrived = lax.all_to_all(outgoing, "expert", split_axis=0, concat_axis=0, tiled=True).reshape(
        slot_count, width_local
    )
    gate_local = w_gate[0]
    lift_local = w_up[0]
    down_local = w_down[0]
    piece = lax.all_gather(arrived, "tensor", axis=1, tiled=True)
    gate_val = jnp.dot(piece, gate_local, preferred_element_type=jnp.float32)
    lift_val = jnp.dot(piece, lift_local, preferred_element_type=jnp.float32)
    hidden = (jax.nn.silu(gate_val) * lift_val).astype(jnp.bfloat16)
    summed = lax.psum_scatter(
        lax.dot_general(
            down_local, hidden, (((0,), (1,)), ((), ())), preferred_element_type=jnp.float32
        ),
        "tensor",
        scatter_dimension=0,
        tiled=True,
    )
    expert_out = summed.astype(jnp.bfloat16).reshape(width_local, expert_count, capacity)
    returned = lax.all_to_all(
        expert_out, "expert", split_axis=1, concat_axis=1, tiled=True
    ).reshape(width_local, slot_count)
    mixed = lax.dot_general(
        dispatch_map, returned, (((0,), (1,)), ((), ())), preferred_element_type=jnp.float32
    )
    return mixed.astype(jnp.bfloat16)


def solution(mesh):
    return jax.shard_map(
        on_device,
        mesh=mesh,
        in_specs=(
            P("expert", "tensor"),
            P("expert"),
            P("expert", None),
            P("expert", None, "tensor"),
            P("expert", None, "tensor"),
            P("expert", "tensor", None),
        ),
        out_specs=P("expert", "tensor"),
        check_vma=False,
    )
```

profile of v0, /device:TPU:0, one launch (start us, length us, event | category | flops | bytes accessed | tf_op | source)
XLA Modules:
  0.0 129.1 jit_solution(3579600606160409925)
XLA Ops:
  6.5 0.0 all-gather.2.cloned.1.call-start
  6.5 0.7 add_divide_fusion
  7.2 0.7 fusion.20
  7.9 0.6 reduce-window.6
  8.5 0.2 slice_reduce_fusion
  8.7 0.8 fusion.19
  9.5 0.7 multiply_add_fusion
  10.2 1.4 %convolution_convert_fusion = bf16[320,640]{1,0:T(8,128)(2,1)S(1)} fusion(bf16[256,640]{1,0:T(8,128)(2,1)} %param.6, f32[256]{0:T(256)S(1)} %add_divide_fusion, s32[256]{0:T(256)S(1)} %multiply_add_fusion), kind=kOutput, calls=%fused_computation.9 | convolution fusion | flops 105635840 | bytes 739328 | tf_op jit(solution)/shard_map/dot_general | solution.py:24
  11.6 19.6 %all_to_all.10 = bf16[8,40,640]{2,1,0:T(8,128)(2,1)} all-to-all(bf16[8,40,640]{2,1,0:T(8,128)(2,1)S(1)} %bitcast.37), channel_id=1, replica_groups=mesh['expert'=8,'tensor'=4] {'expert'}, dimensions={0} | all-to-all | bytes 819200 | tf_op jit(solution)/shard_map/all_to_all | solution.py:28
  31.1 0.0 all-gather.2.cloned.1.call-update
  31.2 0.0 reduce-scatter.2.cloned.1.call-start
  31.2 18.8 %all-gather.2.cloned.1.call-done = bf16[320,2560]{1,0:T(8,128)(2,1)} async-done(((bf16[320,640]{1,0:T(8,128)(2,1)}), bf16[320,2560]{1,0:T(8,128)(2,1)}) %all-gather.2.cloned.1.call-update) | async-done | bytes 1638416 | tf_op jit(solution)/shard_map/all_gather | solution.py:34
  50.0 5.0 %fusion.4 = f32[320,1024]{1,0:T(8,128)S(1)} fusion(bf16[320,2560]{1,0:T(8,128)(2,1)} %all-gather.2.cloned.1.call-done, bf16[1,2560,1024]{2,1,0:T(8,128)(2,1)} %param.9), kind=kOutput, calls=%fused_computation.4 | convolution fusion | flops 1677721600 | bytes 8192000 | tf_op jit(solution)/shard_map/dot_general | solution.py:35
  55.0 0.0 copy-done
  55.0 0.0 slice-start.1
  55.0 4.7 %fusion.12 = bf16[320,1024]{1,0:T(8,128)(2,1)S(1)} fusion(bf16[320,2560]{1,0:T(8,128)(2,1)S(1)} %copy-done, bf16[1,2560,1024]{2,1,0:T(8,128)(2,1)} %param.10, f32[320,1024]{1,0:T(8,128)S(1)} %fusion.4), kind=kOutput, calls=%fused_computation.8 | convolution fusion | flops 1679687680 | bytes 8847360 | tf_op jit(solution)/shard_map/dot_general | solution.py:36
  59.7 0.0 slice-done
  59.7 0.0 slice-done.1
  59.7 3.6 %fusion.6 = f32[2560,320]{0,1:T(8,128)} fusion(bf16[320,1024]{1,0:T(8,128)(2,1)S(1)} %fusion.12, bf16[1,1024,2560]{2,1,0:T(8,128)(2,1)S(1)} %bitcast.43), kind=kOutput, calls=%fused_computation.6 | convolution fusion | flops 1677721600 | bytes 9175040 | tf_op jit(solution)/shard_map/dot_general | solution.py:39
  63.3 0.0 reduce-scatter.2.cloned.1.call-update
  63.3 38.9 %reduce-scatter.2.cloned.1.call-done = f32[640,320]{0,1:T(8,128)} async-done(((f32[2560,320]{0,1:T(8,128)}), f32[640,320]{0,1:T(8,128)}) %reduce-scatter.2.cloned.1.call-update) | async-done | bytes 819216 | tf_op jit(solution)/shard_map/reduce_scatter | solution.py:38
  102.2 1.2 convert_element_type.32
  103.4 17.7 %all_to_all.11 = bf16[640,8,40]{0,2,1:T(8,128)(2,1)S(1)} all-to-all(bf16[640,8,40]{0,2,1:T(8,128)(2,1)S(1)} %bitcast.38), channel_id=1, replica_groups=mesh['expert'=8,'tensor'=4] {'expert'}, dimensions={1} | all-to-all | bytes 819200 | tf_op jit(solution)/shard_map/all_to_all | solution.py:47
  121.1 1.1 convolution_convert_fusion.1
  (5 shorter events, 0.0 us)
Async XLA Ops:
  6.5 43.5 %all-gather.2.cloned.1.call-start = ((), (), s32[]{:S(2)}) async-start(), calls=%async_computation.3 | async-start | bytes 2048000 | tf_op jit(solution)/shard_map/all_gather | solution.py:34
  31.2 71.0 %reduce-scatter.2.cloned.1.call-start = ((), (), s32[]{:S(2)}) async-start(), calls=%async_computation.4 | async-start | bytes 4096000 | tf_op jit(solution)/shard_map/reduce_scatter | solution.py:38
  50.0 5.0 %copy-start = (bf16[320,2560]{1,0:T(8,128)(2,1)S(1)}, bf16[320,2560]{1,0:T(8,128)(2,1)}, u32[]{:S(2)}) copy-start(bf16[320,2560]{1,0:T(8,128)(2,1)} %all-gather.2.cloned.1.call-done) | copy-start | bytes 4915204
  50.0 9.7 %slice-start = ((s8[5242880]{0:T(1024)(128)(4,1)}), s8[4194304]{0:T(1024)(128)(4,1)S(1)}, s32[]{:S(2)}) async-start(s8[5242880]{0:T(1024)(128)(4,1)} %bitcast.42), calls=%async_computation.5 | async-start | bytes 8388608
  55.0 4.7 %slice-start.1 = ((s8[5242880]{0:T(1024)(128)(4,1)}), s8[1048576]{0:T(1024)(128)(4,1)S(1)}, s32[]{:S(2)}) async-start(s8[5242880]{0:T(1024)(128)(4,1)} %bitcast.42), calls=%async_computation.6 | async-start | bytes 2097152
Sparse Core Ops, SparseCore 0:
  31.3 18.6 all-gather.1
  63.4 38.7 reduce-scatter.1
where the time goes:
time: 129 us
  waiting for transfers between devices  57.7 us (45%)
  blocking collectives  37.3 us (29%)
  matrix products  15.7 us (12%)
  between operations  13.5 us (10%)
  other arithmetic  4.63 us (4%)
    reduce_scatter x1, waiting for transfers between devices, on_device(): lax.psum_scatter(lax.dot_general(down_local, hidden, (((0,), (1,)), ((),...  38.9 us
    all_to_all x1, blocking collectives, on_device(): lax.all_to_all(outgoing, 'expert', split_axis=0, concat_axis=0, tiled=True)  19.6 us
    all_gather x1, waiting for transfers between devices, on_device(): piece = lax.all_gather(arrived, 'tensor', axis=1, tiled=True)  18.8 us
    all_to_all x1, blocking collectives, on_device(): lax.all_to_all(expert_out, 'expert', split_axis=1, concat_axis=1, tiled=T...  17.7 us
    dot_general x1, matrix products, on_device(): gate_val = jnp.dot(piece, gate_local, preferred_element_type=jnp.float32)  4.98 us
    dot_general x1, matrix products, on_device(): lift_val = jnp.dot(piece, lift_local, preferred_element_type=jnp.float32)  4.68 us
    dot_general x1, matrix products, on_device(): lax.dot_general(down_local, hidden, (((0,), (1,)), ((), ())), preferred_e...  3.56 us
  transfers between devices with their start and end apart: 2, of which 2 were waited for; matrix products, arithmetic and copies ran while one was open for 0% of the time, Pallas kernels for 0%

commit v1 on v0

--- a/solution.py
+++ b/solution.py
@@ -1,13 +1,319 @@
+import functools
+
 import jax
 import jax.numpy as jnp
 from jax import lax
+from jax.experimental import pallas as pl
+from jax.experimental.pallas import tpu as pltpu
 from jax.sharding import PartitionSpec as P
+
+MESH = pl.DeviceIdType.MESH
+F32 = jnp.float32
+BF16 = jnp.bfloat16
+
+
+def plan(width, cap):
+    chunks, off, row = [], 0, 0
+    while off < width:
+        lanes = min(256, width - off)
+        rows = -(-(cap * (lanes // 128)) // 16) * 16
+        chunks.append((off, lanes, row, rows))
+        off, row = off + lanes, row + rows
+    return chunks, row
+
+
+def pack(block, lanes, rows):
+    parts = [block[:, i : i + 128] for i in range(0, lanes, 128)]
+    spare = rows - block.shape[0] * len(parts)
+    if spare:
+        parts.append(jnp.zeros((spare, 128), F32))
+    return jnp.concatenate(parts, axis=0) if len(parts) > 1 else parts[0]
+
+
+def unpack(packed, lanes, cap):
+    packed = packed.astype(F32)
+    parts = [packed[i * cap : (i + 1) * cap] for i in range(lanes // 128)]
+    return jnp.concatenate(parts, axis=1) if len(parts) > 1 else parts[0]
+
+
+def kernel(
+    n_exp, n_ten, cap, chunks,
+    tokens, logit, ids, w_gate, w_up, w_down,
+    out,
+    wg, wu, wd, send_d, recv_d, send_r, recv_r, x, acc_g, acc_u, hidden, combine,
+    far_out, far_in, near_out, near_in, near_own, half_out, half_in,
+    w_sem, ds_sem, dr_sem, rs_sem, rr_sem, sib_s, sib_r, x_s, x_r, fw_s, fw_r,
+    far_s, far_r, near_s, near_r, half_s, half_r,
+):
+    g = lax.axis_index("expert")
+    t = lax.axis_index("tensor")
+    sib = t + 1 - 2 * lax.rem(t, 2)
+    across = lax.rem(t + 2, 4)
+    diag = lax.rem(sib + 2, 4)
+    tok, width = tokens.shape
+    slots = n_exp * cap
+    n_ff = wg.shape[2]
+    order = list(range(1, n_exp))
+
+    loads = []
+    for s in range(n_ten):
+        loads.append(pltpu.make_async_copy(w_gate.at[0, pl.ds(s * width, width)], wg.at[s], w_sem.at[0, s]))
+        loads.append(pltpu.make_async_copy(w_up.at[0, pl.ds(s * width, width)], wu.at[s], w_sem.at[1, s]))
+    for s in range(n_ten):
+        loads.append(
+            pltpu.make_async_copy(w_down.at[0, :, pl.ds(s * width, width)], wd.at[s], w_sem.at[2, s])
+        )
+    for load in loads:
+        load.start()
+
+    barrier = pltpu.get_barrier_semaphore()
+    for k in order:
+        pl.semaphore_signal(barrier, inc=1, device_id=(lax.rem(g + k, n_exp), t), device_id_type=MESH)
+    for peer in (sib, across):
+        pl.semaphore_signal(barrier, inc=1, device_id=(g, peer), device_id_type=MESH)
+
+    ids_row = ids[...]
+    one_hot = lax.broadcasted_iota(jnp.int32, (n_exp, tok), 0) == ids_row
+    older = lax.broadcasted_iota(jnp.int32, (tok, tok), 0)
+    newer = lax.broadcasted_iota(jnp.int32, (tok, tok), 1)
+    before = jnp.where(older < newer, 1.0, 0.0).astype(BF16)
+    hot = jnp.where(one_hot, 1.0, 0.0)
+    earlier = jnp.dot(hot.astype(BF16), before, preferred_element_type=F32)
+    position = jnp.sum(earlier * hot, axis=0, keepdims=True)
+    dest = ids_row.astype(F32) * float(cap) + position
+    eye = older == newer
+    dest_col = jnp.sum(jnp.where(eye, dest, 0.0), axis=1, keepdims=True)
+    slot_row = lax.broadcasted_iota(jnp.int32, (slots, tok), 0).astype(F32)
+    dispatch = jnp.where(slot_row == dest, 1.0, 0.0).astype(BF16)
+    slot_col = lax.broadcasted_iota(jnp.int32, (tok, slots), 1).astype(F32)
+    combine[...] = jnp.where(slot_col == dest_col, 1.0, 0.0).astype(BF16)
+    factor = jnp.sum(jnp.where(eye, jax.nn.sigmoid(logit[...]), 0.0), axis=1, keepdims=True)
+
+    def exchange(c, src, dst, s_sem, r_sem):
+        _, _, row, rows = chunks[c]
+        copies = []
+        for k in order:
+            e = lax.rem(g + k, n_exp)
+            copies.append(
+                pltpu.make_async_remote_copy(
+                    src_ref=src.at[e, pl.ds(row, rows)],
+                    dst_ref=dst.at[g, pl.ds(row, rows)],
+                    send_sem=s_sem.at[k, c],
+                    recv_sem=r_sem.at[k, c],
+                    device_id=(e, t),
+                    device_id_type=MESH,
+                )
+            )
+        return copies
+
+    def to_tensor(src, dst, s_sem, r_sem, peer):
+        return pltpu.make_async_remote_copy(
+            src_ref=src, dst_ref=dst, send_sem=s_sem, recv_sem=r_sem, device_id=(g, peer), device_id_type=MESH
+        )
+
+    sends = []
+    dispatches = []
+    for c, (off, lanes, row, rows) in enumerate(chunks):
+        scaled = (factor * tokens[:, off : off + lanes].astype(F32)).astype(BF16)
+        outgoing = jnp.dot(dispatch, scaled, preferred_element_type=F32)
+        for e in range(n_exp):
+            send_d[e, row : row + rows] = pack(outgoing[e * cap : (e + 1) * cap], lanes, rows).astype(BF16)
+        if c == 0:
+            pl.semaphore_wait(barrier, n_exp - 1 + 2)
+        copies = exchange(c, send_d, recv_d, ds_sem, dr_sem)
+        for copy in copies:
+            copy.start()
+        recv_d[g, row : row + rows] = send_d[g, row : row + rows]
+        dispatches.append(copies)
+        sends += copies
+
+    crossing, sides = [], []
+    for c, (off, lanes, row, rows) in enumerate(chunks):
+        for copy in dispatches[c]:
+            copy.wait_recv()
+        x[t, :, off : off + lanes] = jnp.concatenate(
+            [unpack(recv_d[e, row : row + rows], lanes, cap) for e in range(n_exp)], axis=0
+        ).astype(BF16)
+        part = x.at[t, :, pl.ds(off, lanes)]
+        crossing.append(to_tensor(part, part, x_s.at[c], x_r.at[c], across))
+        sides.append(to_tensor(part, part, sib_s.at[c], sib_r.at[c], sib))
+        crossing[-1].start()
+        sides[-1].start()
+    sends += crossing + sides
+
+    forwards = []
+
+    def forward(c):
+        off, lanes, _, _ = chunks[c]
+        crossing[c].wait_recv()
+        part = x.at[across, :, pl.ds(off, lanes)]
+        forwards.append(to_tensor(part, part, fw_s.at[c], fw_r.at[c], sib))
+        forwards[-1].start()
+
+    def project(s, first, last):
+        @pl.loop(0, n_ff // 256)
+        def _(n):
+            cols = pl.ds(pl.multiple_of(n * 256, 256), 256)
+            rows_in = x[s]
+            gate = jnp.dot(rows_in, wg[s, :, cols], preferred_element_type=F32)
+            lift = jnp.dot(rows_in, wu[s, :, cols], preferred_element_type=F32)
+            if not first:
+                gate = gate + acc_g[:, cols]
+                lift = lift + acc_u[:, cols]
+            if last:
+                hidden[:, cols] = (jax.nn.silu(gate) * lift).astype(BF16)
+            else:
+                acc_g[:, cols] = gate
+                acc_u[:, cols] = lift
+
+    for load in loads:
+        load.wait()
+    n_chunks = len(chunks)
+    forward(0)
+    project(t, True, False)
+    for c in range(1, n_chunks - 1):
+        forward(c)
+    for copy in sides:
+        copy.wait_recv()
+    project(sib, False, False)
+    forward(n_chunks - 1)
+    project(across, False, False)
+    for copy in forwards:
+        copy.wait_recv()
+    project(diag, False, True)
+    sends += forwards
+
+    def partial(s, c):
+        off, lanes, _, _ = chunks[c]
+        return jnp.dot(hidden[...], wd[s, :, off : off + lanes], preferred_element_type=F32)
+
+    halves = []
+
+    def half(c, copy, mine):
+        off, lanes, _, _ = chunks[c]
+        copy.wait_recv()
+        half_out[:, off : off + lanes] = (mine + far_in[:, off : off + lanes]).astype(BF16)
+        halves.append(
+            to_tensor(
+                half_out.at[:, pl.ds(off, lanes)], half_in.at[:, pl.ds(off, lanes)],
+                half_s.at[c], half_r.at[c], across,
+            )
+        )
+        halves[-1].start()
+        sends.append(halves[-1])
+
+    for c, (off, lanes, _, _) in enumerate(chunks):
+        far_out[:, off : off + lanes] = partial(diag, c)
+        copy = to_tensor(
+            far_out.at[:, pl.ds(off, lanes)], far_in.at[:, pl.ds(off, lanes)], far_s.at[c], far_r.at[c], sib
+        )
+        copy.start()
+        sends.append(copy)
+        half(c, copy, partial(across, c))
+
+    nears = []
+    for c, (off, lanes, _, _) in enumerate(chunks):
+        near_out[:, off : off + lanes] = partial(sib, c)
+        copy = to_tensor(
+            near_out.at[:, pl.ds(off, lanes)], near_in.at[:, pl.ds(off, lanes)], near_s.at[c], near_r.at[c], sib
+        )
+        copy.start()
+        nears.append(copy)
+        near_own[:, off : off + lanes] = partial(t, c)
+    sends += nears
+
+    returns = []
+    for c, (off, lanes, row, rows) in enumerate(chunks):
+        nears[c].wait_recv()
+        halves[c].wait_recv()
+        total = (
+            near_own[:, off : off + lanes] + near_in[:, off : off + lanes] + half_in[:, off : off + lanes].astype(F32)
+        )
+        for e in range(n_exp):
+            send_r[e, row : row + rows] = pack(total[e * cap : (e + 1) * cap], lanes, rows).astype(BF16)
+        copies = exchange(c, send_r, recv_r, rs_sem, rr_sem)
+        for copy in copies:
+            copy.start()
+        recv_r[g, row : row + rows] = send_r[g, row : row + rows]
+        returns.append(copies)
+        sends += copies
+
+    for c, (off, lanes, row, rows) in enumerate(chunks):
+        for copy in returns[c]:
+            copy.wait_recv()
+        returned = jnp.concatenate(
+            [unpack(recv_r[e, row : row + rows], lanes, cap) for e in range(n_exp)], axis=0
+        ).astype(BF16)
+        out[:, off : off + lanes] = jnp.dot(combine[...], returned, preferred_element_type=F32).astype(BF16)
+
+    for copy in sends:
+        copy.wait_send()
+
+
+def fused(tokens, route_logit, expert_ids, w_gate, w_up, w_down):
+    n_exp = lax.axis_size("expert")
+    n_ten = lax.axis_size("tensor")
+    tok, width = tokens.shape
+    n_ff = w_gate.shape[2]
+    cap = 5 * tok // (4 * n_exp)
+    slots = n_exp * cap
+    chunks, block_rows = plan(width, cap)
+    n_c = len(chunks)
+    dma = pltpu.SemaphoreType.DMA
+    vmem = pltpu.VMEM
+    blocks = (n_exp, block_rows, 128)
+    return pl.pallas_call(
+        functools.partial(kernel, n_exp, n_ten, cap, chunks),
+        out_shape=jax.ShapeDtypeStruct((tok, width), BF16),
+        in_specs=[pl.BlockSpec(memory_space=vmem)] * 3 + [pl.BlockSpec(memory_space=pl.ANY)] * 3,
+        out_specs=pl.BlockSpec(memory_space=vmem),
+        scratch_shapes=[
+            vmem((n_ten, width, n_ff), BF16),
+            vmem((n_ten, width, n_ff), BF16),
+            vmem((n_ten, n_ff, width), BF16),
+            vmem(blocks, BF16),
+            vmem(blocks, BF16),
+            vmem(blocks, BF16),
+            vmem(blocks, BF16),
+            vmem((n_ten, slots, width), BF16),
+            vmem((slots, n_ff), F32),
+            vmem((slots, n_ff), F32),
+            vmem((slots, n_ff), BF16),
+            vmem((tok, slots), BF16),
+            vmem((slots, width), F32),
+            vmem((slots, width), F32),
+            vmem((slots, width), F32),
+            vmem((slots, width), F32),
+            vmem((slots, width), F32),
+            vmem((slots, width), BF16),
+            vmem((slots, width), BF16),
+            dma((3, n_ten)),
+        ]
+        + [dma((n_exp, n_c))] * 4
+        + [dma((n_c,))] * 12,
+        compiler_params=pltpu.CompilerParams(
+            collective_id=0, has_side_effects=True, vmem_limit_bytes=48 * 1024 * 1024
+        ),
+        cost_estimate=pl.CostEstimate(
+            flops=6 * slots * n_ten * width * n_ff,
+            bytes_accessed=6 * n_ten * width * n_ff,
+            transcendentals=slots * n_ff,
+        ),
+    )(tokens, route_logit.reshape(1, tok), expert_ids.reshape(1, tok), w_gate, w_up, w_down)
 
 
 def on_device(tokens, route_logit, expert_ids, w_gate, w_up, w_down):
     expert_count = lax.axis_size("expert")
     tok_rows, width_local = tokens.shape
     capacity = 5 * tok_rows // (4 * expert_count)
+    if (
+        lax.axis_size("tensor") == 4
+        and capacity % 8 == 0
+        and width_local % 128 == 0
+        and w_gate.shape[2] % 256 == 0
+        and expert_count <= 8
+    ):
+        return fused(tokens, route_logit, expert_ids, w_gate, w_up, w_down)
     slot_count = expert_count * capacity
     route = expert_ids[:, 0]
     one_hot = (route[:, None] == jnp.arange(expert_count, dtype=jnp.int32)[None, :]).astype(

time: 129 us -> 53.9 us (0.42)
  waiting for transfers between devices: 57.7 us -> 0 us
  Pallas kernels: 0 us -> 48.1 us
  blocking collectives: 37.3 us -> 0 us
  matrix products: 15.7 us -> 0 us
  between operations: 13.5 us -> 0.01 us
  local copies, waits for them, and re-layouts: 0.23 us -> 5.54 us
  other arithmetic: 4.63 us -> 0 us
    pallas_call x0 -> x1, Pallas kernels: none -> 48.1 us  [fused(): pl.pallas_call(functools.partial(kernel, n_exp, n_ten, cap, chunks), out_...]
    reduce_scatter x1 -> x0, waiting for transfers between devices: 38.9 us -> none  [on_device(): lax.psum_scatter(lax.dot_general(down_local, hidden, (((0,), (1,)), ((),...]
    all_to_all x2 -> x0, blocking collectives: 37.3 us -> none  [the longest x1 19.6 us: on_device(): lax.all_to_all(outgoing, 'expert', split_axis=0, concat_axis=0, tiled=True)]
    all_gather x1 -> x0, waiting for transfers between devices: 18.8 us -> none  [on_device(): piece = lax.all_gather(arrived, 'tensor', axis=1, tiled=True)]
    dot_general x5 -> x0, matrix products: 15.7 us -> none  [the longest x1 4.98 us: on_device(): gate_val = jnp.dot(piece, gate_local, preferred_element_type=jnp.float32)]
    unnamed x6 -> x9, local copies, waits for them, and re-layouts: 0.02 us -> 5.54 us
    convert_element_type x2 -> x0, other arithmetic: 1.88 us -> none  [the longest x1 1.19 us: on_device(): summed.astype(jnp.bfloat16).reshape(width_local, expert_count, capacity)]
  transfers between devices with their start and end apart: 2 -> 0, of which waited for: 2 -> 0; matrix products, arithmetic and copies ran while one was open for 0% -> 0% of each run, Pallas kernels for 0% -> 0%
where the time goes in v1:
time: 53.9 us; the launch traced here: 53.7 us
  Pallas kernels  48.1 us (89%)
  local copies, waits for them, and re-layouts  5.54 us (10%)
    pallas_call x1, Pallas kernels, fused(): pl.pallas_call(functools.partial(kernel, n_exp, n_ten, cap, chunks), out_...  48.1 us
    unnamed x9, local copies, waits for them, and re-layouts  5.54 us

profile of v1, /device:TPU:0, one launch (start us, length us, event | category | flops | bytes accessed | tf_op | source)
XLA Modules:
  0.0 53.7 jit_solution(1269388315488089129)
XLA Ops:
  0.0 0.0 copy-start
  0.0 2.5 %copy-done = bf16[1,2560,1024]{2,1,0:T(8,128)(2,1)S(1)} copy-done((bf16[1,2560,1024]{2,1,0:T(8,128)(2,1)S(1)}, bf16[1,2560,1024]{2,1,0:T(8,128)(2,1)}, u32[]{:S(2)}) %copy-start) | copy-done | bytes 5242904
  2.5 0.0 copy-start.1
  2.5 1.0 %copy-done.1 = bf16[256,640]{1,0:T(8,128)(2,1)S(1)} copy-done((bf16[256,640]{1,0:T(8,128)(2,1)S(1)}, bf16[256,640]{1,0:T(8,128)(2,1)}, u32[]{:S(2)}) %copy-start.1) | copy-done | bytes 327704
  3.5 0.0 copy-start.2
  3.5 0.7 %copy-done.2 = f32[256]{0:T(256)S(1)} copy-done((f32[256]{0:T(256)S(1)}, f32[256]{0:T(256)}, u32[]{:S(2)}) %copy-start.2) | copy-done | bytes 1048
  4.1 0.0 copy-start.3
  4.1 0.7 %copy-done.3 = s32[256,1]{0,1:T(1,128)S(1)} copy-done((s32[256,1]{0,1:T(1,128)S(1)}, s32[256,1]{0,1:T(1,128)}, u32[]{:S(2)}) %copy-start.3) | copy-done | bytes 1048
  4.8 48.1 %shard_map.64 = bf16[256,640]{1,0:T(8,128)(2,1)S(1)} custom-call(bf16[256,640]{1,0:T(8,128)(2,1)S(1)} %copy-done.1, f32[1,256]{1,0:T(1,128)S(1)} %bitcast.2, s32[1,256]{1,0:T(1,128)S(1)} %bitcast.3, bf16[1,2560,1024]{2,1,0:T(8,128)(2,1)S(1)} %copy-done, bf16[1,2560,1024]{2,1,0:T(8,128)(2,1)} %w_up.1, bf16[1,1024,2560]{2,1,0:T(8,128)(2,1)} %w_down.1), custom_call_target="tpu_custom_call" | custom-call | flops 5033164800 | bytes 15728640 | tf_op jit(solution)/shard_map/pallas_call | solution.py:265
  53.0 0.7 %copy.8 = bf16[256,640]{1,0:T(8,128)(2,1)} copy(bf16[256,640]{1,0:T(8,128)(2,1)S(1)} %shard_map.64) | data formatting | bytes 655360
Async XLA Ops:
  0.0 2.5 %copy-start = (bf16[1,2560,1024]{2,1,0:T(8,128)(2,1)S(1)}, bf16[1,2560,1024]{2,1,0:T(8,128)(2,1)}, u32[]{:S(2)}) copy-start(bf16[1,2560,1024]{2,1,0:T(8,128)(2,1)} %w_gate.1) | copy-start | bytes 15728644
  2.5 1.0 %copy-start.1 = (bf16[256,640]{1,0:T(8,128)(2,1)S(1)}, bf16[256,640]{1,0:T(8,128)(2,1)}, u32[]{:S(2)}) copy-start(bf16[256,640]{1,0:T(8,128)(2,1)} %tokens.1) | copy-start | bytes 983044
  3.5 0.7 %copy-start.2 = (f32[256]{0:T(256)S(1)}, f32[256]{0:T(256)}, u32[]{:S(2)}) copy-start(f32[256]{0:T(256)} %param.7) | copy-start | bytes 3076
  4.1 0.7 %copy-start.3 = (s32[256,1]{0,1:T(1,128)S(1)}, s32[256,1]{0,1:T(1,128)}, u32[]{:S(2)}) copy-start(s32[256,1]{0,1:T(1,128)} %param.8) | copy-start | bytes 3076

commit v2 on v1

--- a/solution.py
+++ b/solution.py
@@ -8,6 +8,7 @@
 from jax.sharding import PartitionSpec as P
 
 MESH = pl.DeviceIdType.MESH
+LIMIT = 63 * 1024 * 1024
 F32 = jnp.float32
 BF16 = jnp.bfloat16
 
@@ -38,11 +39,11 @@
 
 def kernel(
     n_exp, n_ten, cap, chunks,
-    tokens, logit, ids, w_gate, w_up, w_down,
+    tokens_in, logit_in, ids_in, w_gate, w_up, w_down,
     out,
-    wg, wu, wd, send_d, recv_d, send_r, recv_r, x, acc_g, acc_u, hidden, combine,
-    far_out, far_in, near_out, near_in, near_own, half_out, half_in,
-    w_sem, ds_sem, dr_sem, rs_sem, rr_sem, sib_s, sib_r, x_s, x_r, fw_s, fw_r,
+    tokens, logit, ids, wg, wu, wd, send_d, recv_d, send_r, recv_r, x, acc_g, acc_u, hidden, combine,
+    far_out, far_in, far_own, near_out, near_in, near_own, half_out, half_in,
+    in_sem, w_sem, ds_sem, dr_sem, rs_sem, rr_sem, sib_s, sib_r, x_s, x_r, fw_s, fw_r,
     far_s, far_r, near_s, near_r, half_s, half_r,
 ):
     g = lax.axis_index("expert")
@@ -55,16 +56,12 @@
     n_ff = wg.shape[2]
     order = list(range(1, n_exp))
 
-    loads = []
-    for s in range(n_ten):
-        loads.append(pltpu.make_async_copy(w_gate.at[0, pl.ds(s * width, width)], wg.at[s], w_sem.at[0, s]))
-        loads.append(pltpu.make_async_copy(w_up.at[0, pl.ds(s * width, width)], wu.at[s], w_sem.at[1, s]))
-    for s in range(n_ten):
-        loads.append(
-            pltpu.make_async_copy(w_down.at[0, :, pl.ds(s * width, width)], wd.at[s], w_sem.at[2, s])
-        )
-    for load in loads:
-        load.start()
+    small = [
+        pltpu.make_async_copy(src, dst, in_sem.at[i])
+        for i, (src, dst) in enumerate(((ids_in, ids), (logit_in, logit), (tokens_in, tokens)))
+    ]
+    for copy in small:
+        copy.start()
 
     barrier = pltpu.get_barrier_semaphore()
     for k in order:
@@ -72,6 +69,7 @@
     for peer in (sib, across):
         pl.semaphore_signal(barrier, inc=1, device_id=(g, peer), device_id_type=MESH)
 
+    small[0].wait()
     ids_row = ids[...]
     one_hot = lax.broadcasted_iota(jnp.int32, (n_exp, tok), 0) == ids_row
     older = lax.broadcasted_iota(jnp.int32, (tok, tok), 0)
@@ -82,11 +80,9 @@
     position = jnp.sum(earlier * hot, axis=0, keepdims=True)
     dest = ids_row.astype(F32) * float(cap) + position
     eye = older == newer
-    dest_col = jnp.sum(jnp.where(eye, dest, 0.0), axis=1, keepdims=True)
     slot_row = lax.broadcasted_iota(jnp.int32, (slots, tok), 0).astype(F32)
     dispatch = jnp.where(slot_row == dest, 1.0, 0.0).astype(BF16)
-    slot_col = lax.broadcasted_iota(jnp.int32, (tok, slots), 1).astype(F32)
-    combine[...] = jnp.where(slot_col == dest_col, 1.0, 0.0).astype(BF16)
+    small[1].wait()
     factor = jnp.sum(jnp.where(eye, jax.nn.sigmoid(logit[...]), 0.0), axis=1, keepdims=True)
 
     def exchange(c, src, dst, s_sem, r_sem):
@@ -111,6 +107,7 @@
             src_ref=src, dst_ref=dst, send_sem=s_sem, recv_sem=r_sem, device_id=(g, peer), device_id_type=MESH
         )
 
+    small[2].wait()
     sends = []
     dispatches = []
     for c, (off, lanes, row, rows) in enumerate(chunks):
@@ -127,8 +124,27 @@
         dispatches.append(copies)
         sends += copies
 
-    crossing, sides = [], []
-    for c, (off, lanes, row, rows) in enumerate(chunks):
+    loads = []
+    for s in range(n_ten):
+        loads.append(pltpu.make_async_copy(w_gate.at[0, pl.ds(s * width, width)], wg.at[s], w_sem.at[0, s]))
+        loads.append(pltpu.make_async_copy(w_up.at[0, pl.ds(s * width, width)], wu.at[s], w_sem.at[1, s]))
+    for s in range(n_ten):
+        loads.append(
+            pltpu.make_async_copy(w_down.at[0, :, pl.ds(s * width, width)], wd.at[s], w_sem.at[2, s])
+        )
+    for load in loads:
+        load.start()
+    gate_loads, down_loads = loads[: 2 * n_ten], loads[2 * n_ten :]
+
+    dest_col = jnp.sum(jnp.where(eye, dest, 0.0), axis=1, keepdims=True)
+    slot_col = lax.broadcasted_iota(jnp.int32, (tok, slots), 1).astype(F32)
+    combine[...] = jnp.where(slot_col == dest_col, 1.0, 0.0).astype(BF16)
+
+    n_chunks = len(chunks)
+    crossing, sides, forwards = [], [], []
+
+    def gather(c):
+        off, lanes, row, rows = chunks[c]
         for copy in dispatches[c]:
             copy.wait_recv()
         x[t, :, off : off + lanes] = jnp.concatenate(
@@ -139,9 +155,6 @@
         sides.append(to_tensor(part, part, sib_s.at[c], sib_r.at[c], sib))
         crossing[-1].start()
         sides[-1].start()
-    sends += crossing + sides
-
-    forwards = []
 
     def forward(c):
         off, lanes, _, _ = chunks[c]
@@ -150,13 +163,20 @@
         forwards.append(to_tensor(part, part, fw_s.at[c], fw_r.at[c], sib))
         forwards[-1].start()
 
-    def project(s, first, last):
-        @pl.loop(0, n_ff // 256)
-        def _(n):
-            cols = pl.ds(pl.multiple_of(n * 256, 256), 256)
-            rows_in = x[s]
-            gate = jnp.dot(rows_in, wg[s, :, cols], preferred_element_type=F32)
-            lift = jnp.dot(rows_in, wu[s, :, cols], preferred_element_type=F32)
+    tile = 512 if n_ff % 512 == 0 else 256
+
+    def project(one, two, c, first, last):
+        off, lanes, _, _ = chunks[c]
+        feats = slice(off, off + lanes)
+        rows_in = jnp.concatenate([x[one, :, feats], x[two, :, feats]], axis=1)
+        for n in range(0, n_ff, tile):
+            cols = slice(n, n + tile)
+
+            def product(w):
+                w_in = jnp.concatenate([w[one, feats, cols], w[two, feats, cols]], axis=0)
+                return jnp.dot(rows_in, w_in, preferred_element_type=F32)
+
+            gate, lift = product(wg), product(wu)
             if not first:
                 gate = gate + acc_g[:, cols]
                 lift = lift + acc_u[:, cols]
@@ -166,64 +186,82 @@
                 acc_g[:, cols] = gate
                 acc_u[:, cols] = lift
 
-    for load in loads:
+    def near_pair(c):
+        sides[c].wait_recv()
+        project(t, sib, c, c == 0, False)
+
+    def far_pair(c):
+        forwards[c].wait_recv()
+        project(across, diag, c, False, c == n_chunks - 1)
+
+    gather(0)
+    for c in range(1, n_chunks):
+        gather(c)
+        if c == 1:
+            for load in gate_loads:
+                load.wait()
+        near_pair(c - 1)
+        forward(c - 1)
+        if c > 1:
+            far_pair(c - 2)
+    near_pair(n_chunks - 1)
+    forward(n_chunks - 1)
+    far_pair(n_chunks - 2)
+    far_pair(n_chunks - 1)
+    sends += crossing + sides + forwards
+    for load in down_loads:
         load.wait()
-    n_chunks = len(chunks)
-    forward(0)
-    project(t, True, False)
-    for c in range(1, n_chunks - 1):
-        forward(c)
-    for copy in sides:
-        copy.wait_recv()
-    project(sib, False, False)
-    forward(n_chunks - 1)
-    project(across, False, False)
-    for copy in forwards:
-        copy.wait_recv()
-    project(diag, False, True)
-    sends += forwards
 
     def partial(s, c):
         off, lanes, _, _ = chunks[c]
         return jnp.dot(hidden[...], wd[s, :, off : off + lanes], preferred_element_type=F32)
 
-    halves = []
-
-    def half(c, copy, mine):
-        off, lanes, _, _ = chunks[c]
-        copy.wait_recv()
-        half_out[:, off : off + lanes] = (mine + far_in[:, off : off + lanes]).astype(BF16)
-        halves.append(
-            to_tensor(
-                half_out.at[:, pl.ds(off, lanes)], half_in.at[:, pl.ds(off, lanes)],
-                half_s.at[c], half_r.at[c], across,
-            )
-        )
-        halves[-1].start()
-        sends.append(halves[-1])
-
-    for c, (off, lanes, _, _) in enumerate(chunks):
+    back = list(range(n_chunks))[::-1]
+    fars, halves, nears = {}, {}, {}
+
+    def start_far(c):
+        off, lanes, _, _ = chunks[c]
         far_out[:, off : off + lanes] = partial(diag, c)
-        copy = to_tensor(
+        fars[c] = to_tensor(
             far_out.at[:, pl.ds(off, lanes)], far_in.at[:, pl.ds(off, lanes)], far_s.at[c], far_r.at[c], sib
         )
-        copy.start()
-        sends.append(copy)
-        half(c, copy, partial(across, c))
-
-    nears = []
-    for c, (off, lanes, _, _) in enumerate(chunks):
+        fars[c].start()
+
+    def start_half(c):
+        off, lanes, _, _ = chunks[c]
+        fars[c].wait_recv()
+        half_out[:, off : off + lanes] = (
+            far_own[:, off : off + lanes] + far_in[:, off : off + lanes]
+        ).astype(BF16)
+        halves[c] = to_tensor(
+            half_out.at[:, pl.ds(off, lanes)], half_in.at[:, pl.ds(off, lanes)], half_s.at[c], half_r.at[c], across
+        )
+        halves[c].start()
+
+    def start_near(c):
+        off, lanes, _, _ = chunks[c]
         near_out[:, off : off + lanes] = partial(sib, c)
-        copy = to_tensor(
+        nears[c] = to_tensor(
             near_out.at[:, pl.ds(off, lanes)], near_in.at[:, pl.ds(off, lanes)], near_s.at[c], near_r.at[c], sib
         )
-        copy.start()
-        nears.append(copy)
+        nears[c].start()
+
+    start_far(back[0])
+    for i, c in enumerate(back):
+        off, lanes, _, _ = chunks[c]
+        far_own[:, off : off + lanes] = partial(across, c)
+        if i + 1 < n_chunks:
+            start_far(back[i + 1])
+        start_half(c)
+    for c in back:
+        start_near(c)
+        off, lanes, _, _ = chunks[c]
         near_own[:, off : off + lanes] = partial(t, c)
-    sends += nears
-
-    returns = []
-    for c, (off, lanes, row, rows) in enumerate(chunks):
+    sends += list(fars.values()) + list(halves.values()) + list(nears.values())
+
+    returns = {}
+    for c in back:
+        off, lanes, row, rows = chunks[c]
         nears[c].wait_recv()
         halves[c].wait_recv()
         total = (
@@ -235,10 +273,11 @@
         for copy in copies:
             copy.start()
         recv_r[g, row : row + rows] = send_r[g, row : row + rows]
-        returns.append(copies)
+        returns[c] = copies
         sends += copies
 
-    for c, (off, lanes, row, rows) in enumerate(chunks):
+    for c in back:
+        off, lanes, row, rows = chunks[c]
         for copy in returns[c]:
             copy.wait_recv()
         returned = jnp.concatenate(
@@ -265,9 +304,12 @@
     return pl.pallas_call(
         functools.partial(kernel, n_exp, n_ten, cap, chunks),
         out_shape=jax.ShapeDtypeStruct((tok, width), BF16),
-        in_specs=[pl.BlockSpec(memory_space=vmem)] * 3 + [pl.BlockSpec(memory_space=pl.ANY)] * 3,
+        in_specs=[pl.BlockSpec(memory_space=pl.ANY)] * 6,
         out_specs=pl.BlockSpec(memory_space=vmem),
         scratch_shapes=[
+            vmem((tok, width), BF16),
+            vmem((1, tok), F32),
+            vmem((1, tok), jnp.int32),
             vmem((n_ten, width, n_ff), BF16),
             vmem((n_ten, width, n_ff), BF16),
             vmem((n_ten, n_ff, width), BF16),
@@ -285,14 +327,16 @@
             vmem((slots, width), F32),
             vmem((slots, width), F32),
             vmem((slots, width), F32),
+            vmem((slots, width), F32),
             vmem((slots, width), BF16),
             vmem((slots, width), BF16),
+            dma((3,)),
             dma((3, n_ten)),
         ]
         + [dma((n_exp, n_c))] * 4
         + [dma((n_c,))] * 12,
         compiler_params=pltpu.CompilerParams(
-            collective_id=0, has_side_effects=True, vmem_limit_bytes=48 * 1024 * 1024
+            collective_id=0, has_side_effects=True, vmem_limit_bytes=LIMIT
         ),
         cost_estimate=pl.CostEstimate(
             flops=6 * slots * n_ten * width * n_ff,

time: 53.9 us -> 45.3 us (0.84)
  Pallas kernels: 48.1 us -> 43.4 us
  local copies, waits for them, and re-layouts: 5.54 us -> 1.73 us
    pallas_call x1, Pallas kernels: 48.1 us -> 43.4 us  [fused(): pl.pallas_call(functools.partial(kernel, n_exp, n_ten, cap, chunks), out_...]
    unnamed x9 -> x1, local copies, waits for them, and re-layouts: 5.54 us -> 1.73 us
where the time goes in v2:
time: 45.3 us; the launch traced here: 45.1 us
  Pallas kernels  43.4 us (96%)
  local copies, waits for them, and re-layouts  1.73 us (4%)
    pallas_call x1, Pallas kernels, fused(): pl.pallas_call(functools.partial(kernel, n_exp, n_ten, cap, chunks), out_...  43.4 us
    unnamed x1, local copies, waits for them, and re-layouts  1.73 us

profile of v2, /device:TPU:0, one launch (start us, length us, event | category | flops | bytes accessed | tf_op | source)
XLA Modules:
  0.0 45.1 jit_solution(9904850915136956495)
XLA Ops:
  0.0 43.4 %shard_map.64 = bf16[256,640]{1,0:T(8,128)(2,1)} custom-call(bf16[256,640]{1,0:T(8,128)(2,1)} %tokens_in.1, f32[1,256]{1,0:T(1,128)} %bitcast.2, s32[1,256]{1,0:T(1,128)} %bitcast.3, bf16[1,2560,1024]{2,1,0:T(8,128)(2,1)} %w_gate.1, bf16[1,2560,1024]{2,1,0:T(8,128)(2,1)} %w_up.1, bf16[1,1024,2560]{2,1,0:T(8,128)(2,1)} %w_down.1), custom_call_target="tpu_custom_call" | custom-call | flops 5033164800 | bytes 15728640 | tf_op jit(solution)/shard_map/pallas_call | solution.py:304
  43.4 1.7 %copy.8 = bf16[256,640]{1,0:T(8,128)(2,1)} copy(bf16[256,640]{1,0:T(8,128)(2,1)} %shard_map.64) | data formatting | bytes 655360

commit v3 on v0

--- a/solution.py
+++ b/solution.py
@@ -1,13 +1,427 @@
+import functools
+
 import jax
 import jax.numpy as jnp
 from jax import lax
+from jax.experimental import pallas as pl
+from jax.experimental.pallas import tpu as pltpu
 from jax.sharding import PartitionSpec as P
+
+MESH = pl.DeviceIdType.MESH
+LIMIT = 63 * 1024 * 1024
+F32 = jnp.float32
+BF16 = jnp.bfloat16
+
+
+def plan(width, cap):
+    chunks, off, row = [], 0, 0
+    while off < width:
+        lanes = min(256, width - off)
+        rows = -(-(cap * (lanes // 128)) // 16) * 16
+        chunks.append((off, lanes, row, rows))
+        off, row = off + lanes, row + rows
+    return chunks, row
+
+
+def pack(block, lanes, rows):
+    parts = [block[:, i : i + 128] for i in range(0, lanes, 128)]
+    spare = rows - block.shape[0] * len(parts)
+    if spare:
+        parts.append(jnp.zeros((spare, 128), F32))
+    return jnp.concatenate(parts, axis=0) if len(parts) > 1 else parts[0]
+
+
+def unpack(packed, lanes, cap):
+    packed = packed.astype(F32)
+    parts = [packed[i * cap : (i + 1) * cap] for i in range(lanes // 128)]
+    return jnp.concatenate(parts, axis=1) if len(parts) > 1 else parts[0]
+
+
+def cut(cap):
+    first = 24 if cap == 40 else cap
+    return [(0, first)] + ([(first, cap - first)] if cap > first else [])
+
+
+def kernel(n_exp, n_ten, cap, batches, plans, names, *refs):
+    r = dict(zip(names, refs))
+    tokens, logit, ids = r["tokens"], r["logit"], r["ids"]
+    wg, wu, wd, combine, out = r["wg"], r["wu"], r["wd"], r["combine"], r["out"]
+    w_sem = r["w_sem"]
+    g = lax.axis_index("expert")
+    t = lax.axis_index("tensor")
+    sib = t + 1 - 2 * lax.rem(t, 2)
+    across = lax.rem(t + 2, 4)
+    diag = lax.rem(sib + 2, 4)
+    tok, width = tokens.shape
+    n_ff = wg.shape[2]
+    n_chunks = len(plans[0])
+    tile = 512 if n_ff % 512 == 0 else 256
+    order = list(range(1, n_exp))
+    all_b = range(len(batches))
+
+    small = [
+        pltpu.make_async_copy(r[name + "_in"], r[name], r["in_sem"].at[i])
+        for i, name in enumerate(("ids", "logit", "tokens"))
+    ]
+    for copy in small:
+        copy.start()
+
+    barrier = pltpu.get_barrier_semaphore()
+    for k in order:
+        pl.semaphore_signal(barrier, inc=1, device_id=(lax.rem(g + k, n_exp), t), device_id_type=MESH)
+    for peer in (sib, across):
+        pl.semaphore_signal(barrier, inc=1, device_id=(g, peer), device_id_type=MESH)
+
+    small[0].wait()
+    ids_row = ids[...]
+    one_hot = lax.broadcasted_iota(jnp.int32, (n_exp, tok), 0) == ids_row
+    older = lax.broadcasted_iota(jnp.int32, (tok, tok), 0)
+    newer = lax.broadcasted_iota(jnp.int32, (tok, tok), 1)
+    before = jnp.where(older < newer, 1.0, 0.0).astype(BF16)
+    hot = jnp.where(one_hot, 1.0, 0.0)
+    earlier = jnp.dot(hot.astype(BF16), before, preferred_element_type=F32)
+    position = jnp.sum(earlier * hot, axis=0, keepdims=True)
+    dest = ids_row.astype(F32) * float(cap) + position
+    eye = older == newer
+    dispatch = []
+    for first, rows in batches:
+        row = lax.broadcasted_iota(jnp.int32, (rows, tok), 0)
+        slot = jnp.concatenate([row + (e * cap + first) for e in range(n_exp)], axis=0).astype(F32)
+        dispatch.append(jnp.where(slot == dest, 1.0, 0.0).astype(BF16))
+    small[1].wait()
+    factor = jnp.sum(jnp.where(eye, jax.nn.sigmoid(logit[...]), 0.0), axis=1, keepdims=True)
+
+    def exchange(b, c, kind):
+        _, _, row, rows = plans[b][c]
+        src, dst = r["send_" + kind][b], r["recv_" + kind][b]
+        copies = []
+        for k in order:
+            e = lax.rem(g + k, n_exp)
+            copies.append(
+                pltpu.make_async_remote_copy(
+                    src_ref=src.at[e, pl.ds(row, rows)],
+                    dst_ref=dst.at[g, pl.ds(row, rows)],
+                    send_sem=r["s_" + kind].at[b, k, c],
+                    recv_sem=r["r_" + kind].at[b, k, c],
+                    device_id=(e, t),
+                    device_id_type=MESH,
+                )
+            )
+        return copies
+
+    def to_tensor(src, dst, kind, b, c, peer):
+        return pltpu.make_async_remote_copy(
+            src_ref=src,
+            dst_ref=dst,
+            send_sem=r["s_" + kind].at[b, c],
+            recv_sem=r["r_" + kind].at[b, c],
+            device_id=(g, peer),
+            device_id_type=MESH,
+        )
+
+    def post(b, c, kind, values):
+        _, lanes, row, rows = plans[b][c]
+        n = batches[b][1]
+        src, dst = r["send_" + kind][b], r["recv_" + kind][b]
+        for e in range(n_exp):
+            src[e, row : row + rows] = pack(values[e * n : (e + 1) * n], lanes, rows).astype(BF16)
+        copies = exchange(b, c, kind)
+        if kind == "d" and b == 0 and c == 0:
+            pl.semaphore_wait(barrier, n_exp - 1 + 2)
+        for copy in copies:
+            copy.start()
+        dst[g, row : row + rows] = src[g, row : row + rows]
+        sends.extend(copies)
+        return copies
+
+    def collect(b, c, kind, copies):
+        _, lanes, row, rows = plans[b][c]
+        for copy in copies:
+            copy.wait_recv()
+        src = r["recv_" + kind][b]
+        return jnp.concatenate(
+            [unpack(src[e, row : row + rows], lanes, batches[b][1]) for e in range(n_exp)], axis=0
+        ).astype(BF16)
+
+    sends = []
+    small[2].wait()
+    scaled = (factor * tokens[...].astype(F32)).astype(BF16)
+    dispatches = {}
+    for b in all_b:
+        for c in range(n_chunks):
+            off, lanes, _, _ = plans[b][c]
+            outgoing = jnp.dot(dispatch[b], scaled[:, off : off + lanes], preferred_element_type=F32)
+            dispatches[b, c] = post(b, c, "d", outgoing)
+
+    w_loads, down_loads = [], []
+    for i, s in enumerate((t, sib, across, diag)):
+        rows_of = pl.ds(pl.multiple_of(s * width, 128), width)
+        w_loads.append(pltpu.make_async_copy(r["w_gate"].at[0, rows_of], wg.at[s], w_sem.at[0, i]))
+        w_loads.append(pltpu.make_async_copy(r["w_up"].at[0, rows_of], wu.at[s], w_sem.at[1, i]))
+    for s in range(n_ten):
+        down_loads.append(
+            pltpu.make_async_copy(r["w_down"].at[0, :, pl.ds(s * width, width)], wd.at[s], w_sem.at[2, s])
+        )
+    for load in w_loads + down_loads:
+        load.start()
+
+    dest_col = jnp.sum(jnp.where(eye, dest, 0.0), axis=1, keepdims=True)
+    for b, (first, rows) in enumerate(batches):
+        lane = lax.broadcasted_iota(jnp.int32, (1, n_exp * rows), 1)
+        slot = lane + first
+        for e in range(1, n_exp):
+            slot = slot + jnp.where(lane >= e * rows, cap - rows, 0)
+        combine[b][...] = jnp.where(slot.astype(F32) == dest_col, 1.0, 0.0).astype(BF16)
+
+    crossing, sides, forwards = {}, {}, {}
+
+    def gather(b, c):
+        off, lanes, _, _ = plans[b][c]
+        x = r["x"][b]
+        x[t, :, off : off + lanes] = collect(b, c, "d", dispatches[b, c])
+        part = x.at[t, :, pl.ds(off, lanes)]
+        crossing[b, c] = to_tensor(part, part, "cross", b, c, across)
+        sides[b, c] = to_tensor(part, part, "side", b, c, sib)
+        crossing[b, c].start()
+        sides[b, c].start()
+
+    def forward(b, c):
+        off, lanes, _, _ = plans[b][c]
+        crossing[b, c].wait_recv()
+        part = r["x"][b].at[across, :, pl.ds(off, lanes)]
+        forwards[b, c] = to_tensor(part, part, "fwd", b, c, sib)
+        forwards[b, c].start()
+
+    def project(b, c, one, two, begin, end):
+        off, lanes, _, _ = plans[b][c]
+        x, acc_g, acc_u, hidden = r["x"][b], r["acc_g"][b], r["acc_u"][b], r["hidden"][b]
+        feats = slice(off, off + lanes)
+        rows_in = jnp.concatenate([x[one, :, feats], x[two, :, feats]], axis=1)
+        for n in range(0, n_ff, tile):
+            cols = slice(n, n + tile)
+
+            def product(w):
+                w_in = jnp.concatenate([w[one, feats, cols], w[two, feats, cols]], axis=0)
+                return jnp.dot(rows_in, w_in, preferred_element_type=F32)
+
+            gate, lift = product(wg), product(wu)
+            if not begin:
+                gate = gate + acc_g[:, cols]
+                lift = lift + acc_u[:, cols]
+            if end:
+                hidden[:, cols] = (jax.nn.silu(gate) * lift).astype(BF16)
+            else:
+                acc_g[:, cols] = gate
+                acc_u[:, cols] = lift
+
+    def near_pair(b, c):
+        sides[b, c].wait_recv()
+        project(b, c, t, sib, c == 0, False)
+
+    def far_pair(b, c):
+        forwards[b, c].wait_recv()
+        project(b, c, across, diag, False, c == n_chunks - 1)
+
+    back = list(range(n_chunks))[::-1]
+    fars, halves, nears, returns = {}, {}, {}, {}
+
+    def partial(b, s, c):
+        off, lanes, _, _ = plans[b][c]
+        return jnp.dot(r["hidden"][b][...], wd[s, :, off : off + lanes], preferred_element_type=F32)
+
+    def start_far(b, c):
+        off, lanes, _, _ = plans[b][c]
+        part = pl.ds(off, lanes)
+        r["far_out"][b][:, off : off + lanes] = partial(b, diag, c)
+        fars[b, c] = to_tensor(r["far_out"][b].at[:, part], r["far_in"][b].at[:, part], "far", b, c, sib)
+        fars[b, c].start()
+
+    def start_half(b, c):
+        off, lanes, _, _ = plans[b][c]
+        part, lane = pl.ds(off, lanes), slice(off, off + lanes)
+        fars[b, c].wait_recv()
+        r["half_out"][b][:, lane] = (r["far_own"][b][:, lane] + r["far_in"][b][:, lane]).astype(BF16)
+        halves[b, c] = to_tensor(r["half_out"][b].at[:, part], r["half_in"][b].at[:, part], "half", b, c, across)
+        halves[b, c].start()
+
+    def far_side(b):
+        start_far(b, back[0])
+        for i, c in enumerate(back):
+            off, lanes, _, _ = plans[b][c]
+            r["far_own"][b][:, off : off + lanes] = partial(b, across, c)
+            if i + 1 < n_chunks:
+                start_far(b, back[i + 1])
+            start_half(b, c)
+
+    def near_side(b):
+        for c in back:
+            off, lanes, _, _ = plans[b][c]
+            part = pl.ds(off, lanes)
+            r["near_out"][b][:, off : off + lanes] = partial(b, sib, c)
+            nears[b, c] = to_tensor(r["near_out"][b].at[:, part], r["near_in"][b].at[:, part], "near", b, c, sib)
+            nears[b, c].start()
+            r["near_own"][b][:, off : off + lanes] = partial(b, t, c)
+
+    def give_back(b, c):
+        off, lanes, _, _ = plans[b][c]
+        lane = slice(off, off + lanes)
+        nears[b, c].wait_recv()
+        halves[b, c].wait_recv()
+        total = (
+            r["near_own"][b][:, lane] + r["near_in"][b][:, lane] + r["half_in"][b][:, lane].astype(F32)
+        )
+        returns[b, c] = post(b, c, "r", total)
+
+    last = n_chunks - 1
+
+    def first_batch(b):
+        gather(b, 0)
+        for c in range(1, n_chunks):
+            gather(b, c)
+            if c == 1:
+                for load in w_loads[:4]:
+                    load.wait()
+            near_pair(b, c - 1)
+            forward(b, c - 1)
+            if c > 1:
+                if c == 2:
+                    for load in w_loads[4:]:
+                        load.wait()
+                far_pair(b, c - 2)
+        near_pair(b, last)
+
+    first_batch(0)
+    if len(batches) == 1:
+        forward(0, last)
+        far_pair(0, last - 1)
+        far_pair(0, last)
+        for load in down_loads:
+            load.wait()
+        far_side(0)
+        near_side(0)
+        for c in back:
+            give_back(0, c)
+    else:
+        gather(1, 0)
+        forward(0, last)
+        far_pair(0, last - 1)
+        for c in range(1, n_chunks):
+            gather(1, c)
+        far_pair(0, last)
+        for load in down_loads:
+            load.wait()
+        forward(1, 0)
+        far_side(0)
+        for c in range(1, n_chunks):
+            forward(1, c)
+        near_side(0)
+        for c in range(n_chunks):
+            near_pair(1, c)
+        for c in range(n_chunks):
+            give_back(0, back[c])
+            far_pair(1, c)
+        far_side(1)
+        near_side(1)
+        for c in back:
+            give_back(1, c)
+
+    for c in back:
+        off, lanes, _, _ = plans[0][c]
+        mixed = None
+        for b in all_b:
+            term = jnp.dot(combine[b][...], collect(b, c, "r", returns[b, c]), preferred_element_type=F32)
+            mixed = term if mixed is None else mixed + term
+        out[:, off : off + lanes] = mixed.astype(BF16)
+
+    for group in (crossing, sides, forwards, fars, halves, nears):
+        sends.extend(group.values())
+    for copy in sends:
+        copy.wait_send()
+
+
+def grouped(n_b, single, per_batch, n_exp, n_ten, cap, batches, plans, *refs):
+    refs = list(refs)
+    names, values = [], []
+    for name in single:
+        names.append(name)
+        values.append(refs.pop(0))
+    for name in per_batch:
+        names.append(name)
+        values.append([refs.pop(0) for _ in range(n_b)])
+    kernel(n_exp, n_ten, cap, batches, plans, names, *values)
+
+
+def fused(tokens, route_logit, expert_ids, w_gate, w_up, w_down):
+    n_exp = lax.axis_size("expert")
+    n_ten = lax.axis_size("tensor")
+    tok, width = tokens.shape
+    n_ff = w_gate.shape[2]
+    cap = 5 * tok // (4 * n_exp)
+    slots = n_exp * cap
+    batches = cut(cap)
+    made = [plan(width, rows) for _, rows in batches]
+    plans = [chunks for chunks, _ in made]
+    n_b, n_c = len(batches), len(plans[0])
+    vmem, dma = pltpu.VMEM, pltpu.SemaphoreType.DMA
+    scratch = {
+        "tokens": vmem((tok, width), BF16),
+        "logit": vmem((1, tok), F32),
+        "ids": vmem((1, tok), jnp.int32),
+        "wg": vmem((n_ten, width, n_ff), BF16),
+        "wu": vmem((n_ten, width, n_ff), BF16),
+        "wd": vmem((n_ten, n_ff, width), BF16),
+        "in_sem": dma((3,)),
+        "w_sem": dma((3, n_ten)),
+    }
+    for kind in ("d", "r"):
+        scratch["s_" + kind] = dma((n_b, n_exp, n_c))
+        scratch["r_" + kind] = dma((n_b, n_exp, n_c))
+    for kind in ("cross", "side", "fwd", "far", "half", "near"):
+        scratch["s_" + kind] = dma((n_b, n_c))
+        scratch["r_" + kind] = dma((n_b, n_c))
+    lists = {}
+    for name in ("send_d", "recv_d", "send_r", "recv_r"):
+        lists[name] = [vmem((n_exp, block, 128), BF16) for _, block in made]
+    counts = [n_exp * rows for _, rows in batches]
+    lists["x"] = [vmem((n_ten, n, width), BF16) for n in counts]
+    for name in ("acc_g", "acc_u"):
+        lists[name] = [vmem((n, n_ff), F32) for n in counts]
+    lists["hidden"] = [vmem((n, n_ff), BF16) for n in counts]
+    lists["combine"] = [vmem((tok, n), BF16) for n in counts]
+    for name in ("far_out", "far_in", "far_own", "near_out", "near_in", "near_own"):
+        lists[name] = [vmem((n, width), F32) for n in counts]
+    for name in ("half_out", "half_in"):
+        lists[name] = [vmem((n, width), BF16) for n in counts]
+    single = ["tokens_in", "logit_in", "ids_in", "w_gate", "w_up", "w_down", "out"] + list(scratch)
+    return pl.pallas_call(
+        functools.partial(grouped, n_b, single, list(lists), n_exp, n_ten, cap, batches, plans),
+        out_shape=jax.ShapeDtypeStruct((tok, width), BF16),
+        in_specs=[pl.BlockSpec(memory_space=pl.ANY)] * 6,
+        out_specs=pl.BlockSpec(memory_space=vmem),
+        scratch_shapes=list(scratch.values()) + [ref for group in lists.values() for ref in group],
+        compiler_params=pltpu.CompilerParams(
+            collective_id=0, has_side_effects=True, vmem_limit_bytes=LIMIT
+        ),
+        cost_estimate=pl.CostEstimate(
+            flops=6 * slots * n_ten * width * n_ff,
+            bytes_accessed=6 * n_ten * width * n_ff,
+            transcendentals=slots * n_ff,
+        ),
+    )(tokens, route_logit.reshape(1, tok), expert_ids.reshape(1, tok), w_gate, w_up, w_down)
 
 
 def on_device(tokens, route_logit, expert_ids, w_gate, w_up, w_down):
     expert_count = lax.axis_size("expert")
     tok_rows, width_local = tokens.shape
     capacity = 5 * tok_rows // (4 * expert_count)
+    if (
+        lax.axis_size("tensor") == 4
+        and capacity % 8 == 0
+        and width_local % 128 == 0
+        and w_gate.shape[2] % 256 == 0
+        and expert_count <= 8
+    ):
+        return fused(tokens, route_logit, expert_ids, w_gate, w_up, w_down)
     slot_count = expert_count * capacity
     route = expert_ids[:, 0]
     one_hot = (route[:, None] == jnp.arange(expert_count, dtype=jnp.int32)[None, :]).astype(

time: 129 us -> 48.9 us (0.38)
  waiting for transfers between devices: 57.7 us -> 0 us
  Pallas kernels: 0 us -> 47 us
  blocking collectives: 37.3 us -> 0 us
  matrix products: 15.7 us -> 0 us
  between operations: 13.5 us -> 0.01 us
  other arithmetic: 4.63 us -> 0 us
  local copies, waits for them, and re-layouts: 0.23 us -> 1.73 us
    pallas_call x0 -> x1, Pallas kernels: none -> 47 us  [fused(): pl.pallas_call(functools.partial(grouped, n_b, single, list(lists), n_exp...]
    reduce_scatter x1 -> x0, waiting for transfers between devices: 38.9 us -> none  [on_device(): lax.psum_scatter(lax.dot_general(down_local, hidden, (((0,), (1,)), ((),...]
    all_to_all x2 -> x0, blocking collectives: 37.3 us -> none  [the longest x1 19.6 us: on_device(): lax.all_to_all(outgoing, 'expert', split_axis=0, concat_axis=0, tiled=True)]
    all_gather x1 -> x0, waiting for transfers between devices: 18.8 us -> none  [on_device(): piece = lax.all_gather(arrived, 'tensor', axis=1, tiled=True)]
    dot_general x5 -> x0, matrix products: 15.7 us -> none  [the longest x1 4.98 us: on_device(): gate_val = jnp.dot(piece, gate_local, preferred_element_type=jnp.float32)]
    convert_element_type x2 -> x0, other arithmetic: 1.88 us -> none  [the longest x1 1.19 us: on_device(): summed.astype(jnp.bfloat16).reshape(width_local, expert_count, capacity)]
    unnamed x6 -> x1, local copies, waits for them, and re-layouts: 0.02 us -> 1.73 us
  transfers between devices with their start and end apart: 2 -> 0, of which waited for: 2 -> 0; matrix products, arithmetic and copies ran while one was open for 0% -> 0% of each run, Pallas kernels for 0% -> 0%
where the time goes in v3:
time: 48.9 us; the launch traced here: 48.8 us
  Pallas kernels  47 us (96%)
  local copies, waits for them, and re-layouts  1.73 us (4%)
    pallas_call x1, Pallas kernels, fused(): pl.pallas_call(functools.partial(grouped, n_b, single, list(lists), n_exp...  47 us
    unnamed x1, local copies, waits for them, and re-layouts  1.73 us

profile of v3, /device:TPU:0, one launch (start us, length us, event | category | flops | bytes accessed | tf_op | source)
XLA Modules:
  0.0 48.8 jit_solution(9580091197177600619)
XLA Ops:
  0.0 47.0 %shard_map.64 = bf16[256,640]{1,0:T(8,128)(2,1)} custom-call(bf16[256,640]{1,0:T(8,128)(2,1)} %refs_0_.1, f32[1,256]{1,0:T(1,128)} %bitcast.2, s32[1,256]{1,0:T(1,128)} %bitcast.3, bf16[1,2560,1024]{2,1,0:T(8,128)(2,1)} %refs_3_.1, bf16[1,2560,1024]{2,1,0:T(8,128)(2,1)} %refs_4_.1, bf16[1,1024,2560]{2,1,0:T(8,128)(2,1)} %refs_5_.1), custom_call_target="tpu_custom_call" | custom-call | flops 5033164800 | bytes 15728640 | tf_op jit(solution)/shard_map/pallas_call | solution.py:396
  47.0 1.7 %copy.8 = bf16[256,640]{1,0:T(8,128)(2,1)} copy(bf16[256,640]{1,0:T(8,128)(2,1)} %shard_map.64) | data formatting | bytes 655360

commit v4 on v3

--- a/solution.py
+++ b/solution.py
@@ -38,8 +38,7 @@
 
 
 def cut(cap):
-    first = 24 if cap == 40 else cap
-    return [(0, first)] + ([(first, cap - first)] if cap > first else [])
+    return [(0, cap)]
 
 
 def kernel(n_exp, n_ten, cap, batches, plans, names, *refs):
@@ -71,6 +70,16 @@
         pl.semaphore_signal(barrier, inc=1, device_id=(lax.rem(g + k, n_exp), t), device_id_type=MESH)
     for peer in (sib, across):
         pl.semaphore_signal(barrier, inc=1, device_id=(g, peer), device_id_type=MESH)
+
+    w_loads, down_loads = [], []
+    for i, s in enumerate((t, sib, across, diag)):
+        rows_of = pl.ds(pl.multiple_of(s * width, 128), width)
+        w_loads.append(pltpu.make_async_copy(r["w_gate"].at[0, rows_of], wg.at[s], w_sem.at[0, i]))
+        w_loads.append(pltpu.make_async_copy(r["w_up"].at[0, rows_of], wu.at[s], w_sem.at[1, i]))
+    for s in range(n_ten):
+        down_loads.append(
+            pltpu.make_async_copy(r["w_down"].at[0, :, pl.ds(s * width, width)], wd.at[s], w_sem.at[2, s])
+        )
 
     small[0].wait()
     ids_row = ids[...]
@@ -145,6 +154,8 @@
 
     sends = []
     small[2].wait()
+    for load in w_loads[:4]:
+        load.start()
     scaled = (factor * tokens[...].astype(F32)).astype(BF16)
     dispatches = {}
     for b in all_b:
@@ -153,16 +164,7 @@
             outgoing = jnp.dot(dispatch[b], scaled[:, off : off + lanes], preferred_element_type=F32)
             dispatches[b, c] = post(b, c, "d", outgoing)
 
-    w_loads, down_loads = [], []
-    for i, s in enumerate((t, sib, across, diag)):
-        rows_of = pl.ds(pl.multiple_of(s * width, 128), width)
-        w_loads.append(pltpu.make_async_copy(r["w_gate"].at[0, rows_of], wg.at[s], w_sem.at[0, i]))
-        w_loads.append(pltpu.make_async_copy(r["w_up"].at[0, rows_of], wu.at[s], w_sem.at[1, i]))
-    for s in range(n_ten):
-        down_loads.append(
-            pltpu.make_async_copy(r["w_down"].at[0, :, pl.ds(s * width, width)], wd.at[s], w_sem.at[2, s])
-        )
-    for load in w_loads + down_loads:
+    for load in w_loads[4:] + down_loads:
         load.start()
 
     dest_col = jnp.sum(jnp.where(eye, dest, 0.0), axis=1, keepdims=True)
@@ -209,7 +211,7 @@
                 gate = gate + acc_g[:, cols]
                 lift = lift + acc_u[:, cols]
             if end:
-                hidden[:, cols] = (jax.nn.silu(gate) * lift).astype(BF16)
+                hidden[:, cols] = ((0.5 * gate) * (1.0 + jnp.tanh(0.5 * gate)) * lift).astype(BF16)
             else:
                 acc_g[:, cols] = gate
                 acc_u[:, cols] = lift
@@ -225,16 +227,28 @@
     back = list(range(n_chunks))[::-1]
     fars, halves, nears, returns = {}, {}, {}, {}
 
-    def partial(b, s, c):
-        off, lanes, _, _ = plans[b][c]
-        return jnp.dot(r["hidden"][b][...], wd[s, :, off : off + lanes], preferred_element_type=F32)
+    def partials(b, one, two, c):
+        off, lanes, _, _ = plans[b][c]
+        rows_in, part = r["hidden"][b][...], slice(off, off + lanes)
+        if lanes == 128:
+            both = jnp.dot(
+                rows_in,
+                jnp.concatenate([wd[one, :, part], wd[two, :, part]], axis=1),
+                preferred_element_type=F32,
+            )
+            return (lambda: both[:, :lanes]), (lambda: both[:, lanes:])
+        return tuple(
+            functools.partial(jnp.dot, rows_in, wd[s, :, part], preferred_element_type=F32) for s in (one, two)
+        )
 
     def start_far(b, c):
         off, lanes, _, _ = plans[b][c]
         part = pl.ds(off, lanes)
-        r["far_out"][b][:, off : off + lanes] = partial(b, diag, c)
+        theirs, mine = partials(b, diag, across, c)
+        r["far_out"][b][:, off : off + lanes] = theirs()
         fars[b, c] = to_tensor(r["far_out"][b].at[:, part], r["far_in"][b].at[:, part], "far", b, c, sib)
         fars[b, c].start()
+        r["far_own"][b][:, off : off + lanes] = mine()
 
     def start_half(b, c):
         off, lanes, _, _ = plans[b][c]
@@ -247,8 +261,6 @@
     def far_side(b):
         start_far(b, back[0])
         for i, c in enumerate(back):
-            off, lanes, _, _ = plans[b][c]
-            r["far_own"][b][:, off : off + lanes] = partial(b, across, c)
             if i + 1 < n_chunks:
                 start_far(b, back[i + 1])
             start_half(b, c)
@@ -257,10 +269,11 @@
         for c in back:
             off, lanes, _, _ = plans[b][c]
             part = pl.ds(off, lanes)
-            r["near_out"][b][:, off : off + lanes] = partial(b, sib, c)
+            theirs, mine = partials(b, sib, t, c)
+            r["near_out"][b][:, off : off + lanes] = theirs()
             nears[b, c] = to_tensor(r["near_out"][b].at[:, part], r["near_in"][b].at[:, part], "near", b, c, sib)
             nears[b, c].start()
-            r["near_own"][b][:, off : off + lanes] = partial(b, t, c)
+            r["near_own"][b][:, off : off + lanes] = mine()
 
     def give_back(b, c):
         off, lanes, _, _ = plans[b][c]
@@ -274,56 +287,31 @@
 
     last = n_chunks - 1
 
-    def first_batch(b):
-        gather(b, 0)
-        for c in range(1, n_chunks):
-            gather(b, c)
-            if c == 1:
-                for load in w_loads[:4]:
-                    load.wait()
-            near_pair(b, c - 1)
-            forward(b, c - 1)
-            if c > 1:
-                if c == 2:
-                    for load in w_loads[4:]:
-                        load.wait()
-                far_pair(b, c - 2)
-        near_pair(b, last)
-
-    first_batch(0)
-    if len(batches) == 1:
-        forward(0, last)
-        far_pair(0, last - 1)
-        far_pair(0, last)
-        for load in down_loads:
-            load.wait()
-        far_side(0)
-        near_side(0)
-        for c in back:
-            give_back(0, c)
-    else:
-        gather(1, 0)
-        forward(0, last)
-        far_pair(0, last - 1)
-        for c in range(1, n_chunks):
-            gather(1, c)
-        far_pair(0, last)
-        for load in down_loads:
-            load.wait()
-        forward(1, 0)
-        far_side(0)
-        for c in range(1, n_chunks):
-            forward(1, c)
-        near_side(0)
-        for c in range(n_chunks):
-            near_pair(1, c)
-        for c in range(n_chunks):
-            give_back(0, back[c])
-            far_pair(1, c)
-        far_side(1)
-        near_side(1)
-        for c in back:
-            give_back(1, c)
+    gather(0, 0)
+    for load in w_loads[:4]:
+        load.wait()
+    near_pair(0, 0)
+    for c in range(1, n_chunks):
+        gather(0, c)
+        if c == 1:
+            forward(0, 0)
+        if c < last:
+            near_pair(0, c)
+    for load in w_loads[4:]:
+        load.wait()
+    far_pair(0, 0)
+    for c in range(1, last):
+        forward(0, c)
+    near_pair(0, last)
+    forward(0, last)
+    for c in range(1, n_chunks):
+        far_pair(0, c)
+    for load in down_loads:
+        load.wait()
+    far_side(0)
+    near_side(0)
+    for c in back:
+        give_back(0, c)
 
     for c in back:
         off, lanes, _, _ = plans[0][c]

time: 48.9 us -> 45.5 us (0.930)
  Pallas kernels: 47 us -> 43.6 us
    pallas_call x1, Pallas kernels: 47 us -> 43.6 us  [fused(): pl.pallas_call(functools.partial(grouped, n_b, single, list(lists), n_exp...]
where the time goes in v4:
time: 45.5 us; the launch traced here: 45.4 us
  Pallas kernels  43.6 us (96%)
  local copies, waits for them, and re-layouts  1.73 us (4%)
    pallas_call x1, Pallas kernels, fused(): pl.pallas_call(functools.partial(grouped, n_b, single, list(lists), n_exp...  43.6 us
    unnamed x1, local copies, waits for them, and re-layouts  1.73 us

profile of v4, /device:TPU:0, one launch (start us, length us, event | category | flops | bytes accessed | tf_op | source)
XLA Modules:
  0.0 45.4 jit_solution(10819478387308039866)
XLA Ops:
  0.0 43.6 %shard_map.64 = bf16[256,640]{1,0:T(8,128)(2,1)} custom-call(bf16[256,640]{1,0:T(8,128)(2,1)} %refs_0_.1, f32[1,256]{1,0:T(1,128)} %bitcast.2, s32[1,256]{1,0:T(1,128)} %bitcast.3, bf16[1,2560,1024]{2,1,0:T(8,128)(2,1)} %refs_3_.1, bf16[1,2560,1024]{2,1,0:T(8,128)(2,1)} %refs_4_.1, bf16[1,1024,2560]{2,1,0:T(8,128)(2,1)} %refs_5_.1), custom_call_target="tpu_custom_call" | custom-call | flops 5033164800 | bytes 15728640 | tf_op jit(solution)/shard_map/pallas_call | solution.py:384
  43.7 1.7 %copy.8 = bf16[256,640]{1,0:T(8,128)(2,1)} copy(bf16[256,640]{1,0:T(8,128)(2,1)} %shard_map.64) | data formatting | bytes 655360

commit v5 on v4

--- a/solution.py
+++ b/solution.py
@@ -16,7 +16,7 @@
 def plan(width, cap):
     chunks, off, row = [], 0, 0
     while off < width:
-        lanes = min(256, width - off)
+        lanes = min(384 if width == 640 and off == 0 else 256, width - off)
         rows = -(-(cap * (lanes // 128)) // 16) * 16
         chunks.append((off, lanes, row, rows))
         off, row = off + lanes, row + rows
@@ -230,7 +230,7 @@
     def partials(b, one, two, c):
         off, lanes, _, _ = plans[b][c]
         rows_in, part = r["hidden"][b][...], slice(off, off + lanes)
-        if lanes == 128:
+        if lanes % 256:
             both = jnp.dot(
                 rows_in,
                 jnp.concatenate([wd[one, :, part], wd[two, :, part]], axis=1),

time: 45.5 us -> 49.1 us (1.079)
  Pallas kernels: 43.6 us -> 47.1 us
    pallas_call x1, Pallas kernels: 43.6 us -> 47.1 us  [fused(): pl.pallas_call(functools.partial(grouped, n_b, single, list(lists), n_exp...]
where the time goes in v5:
time: 49.1 us; the launch traced here: 48.9 us
  Pallas kernels  47.1 us (96%)
  local copies, waits for them, and re-layouts  1.73 us (4%)
    pallas_call x1, Pallas kernels, fused(): pl.pallas_call(functools.partial(grouped, n_b, single, list(lists), n_exp...  47.1 us
    unnamed x1, local copies, waits for them, and re-layouts  1.73 us

profile of v5, /device:TPU:0, one launch (start us, length us, event | category | flops | bytes accessed | tf_op | source)
XLA Modules:
  0.0 48.9 jit_solution(822565079376069005)
XLA Ops:
  0.0 47.1 %shard_map.64 = bf16[256,640]{1,0:T(8,128)(2,1)} custom-call(bf16[256,640]{1,0:T(8,128)(2,1)} %refs_0_.1, f32[1,256]{1,0:T(1,128)} %bitcast.2, s32[1,256]{1,0:T(1,128)} %bitcast.3, bf16[1,2560,1024]{2,1,0:T(8,128)(2,1)} %refs_3_.1, bf16[1,2560,1024]{2,1,0:T(8,128)(2,1)} %refs_4_.1, bf16[1,1024,2560]{2,1,0:T(8,128)(2,1)} %refs_5_.1), custom_call_target="tpu_custom_call" | custom-call | flops 5033164800 | bytes 15728640 | tf_op jit(solution)/shard_map/pallas_call | solution.py:384
  47.1 1.7 %copy.8 = bf16[256,640]{1,0:T(8,128)(2,1)} copy(bf16[256,640]{1,0:T(8,128)(2,1)} %shard_map.64) | data formatting | bytes 655360

commit v6 on v5

--- a/solution.py
+++ b/solution.py
@@ -16,7 +16,7 @@
 def plan(width, cap):
     chunks, off, row = [], 0, 0
     while off < width:
-        lanes = min(384 if width == 640 and off == 0 else 256, width - off)
+        lanes = min(256, width - off)
         rows = -(-(cap * (lanes // 128)) // 16) * 16
         chunks.append((off, lanes, row, rows))
         off, row = off + lanes, row + rows
@@ -38,13 +38,14 @@
 
 
 def cut(cap):
-    return [(0, cap)]
+    first = 24 if cap == 40 else cap
+    return [(0, first)] + ([(first, cap - first)] if cap > first else [])
 
 
 def kernel(n_exp, n_ten, cap, batches, plans, names, *refs):
     r = dict(zip(names, refs))
     tokens, logit, ids = r["tokens"], r["logit"], r["ids"]
-    wg, wu, wd, combine, out = r["wg"], r["wu"], r["wd"], r["combine"], r["out"]
+    wg, wu, wd, out = r["wg"], r["wu"], r["wd"], r["out"]
     w_sem = r["w_sem"]
     g = lax.axis_index("expert")
     t = lax.axis_index("tensor")
@@ -92,11 +93,13 @@
     position = jnp.sum(earlier * hot, axis=0, keepdims=True)
     dest = ids_row.astype(F32) * float(cap) + position
     eye = older == newer
-    dispatch = []
+    bases = [n_exp * first for first, _ in batches]
+    parts = []
     for first, rows in batches:
         row = lax.broadcasted_iota(jnp.int32, (rows, tok), 0)
-        slot = jnp.concatenate([row + (e * cap + first) for e in range(n_exp)], axis=0).astype(F32)
-        dispatch.append(jnp.where(slot == dest, 1.0, 0.0).astype(BF16))
+        parts += [row + (e * cap + first) for e in range(n_exp)]
+    slot = jnp.concatenate(parts, axis=0).astype(F32)
+    dispatch = jnp.where(slot == dest, 1.0, 0.0).astype(BF16)
     small[1].wait()
     factor = jnp.sum(jnp.where(eye, jax.nn.sigmoid(logit[...]), 0.0), axis=1, keepdims=True)
 
@@ -158,11 +161,11 @@
         load.start()
     scaled = (factor * tokens[...].astype(F32)).astype(BF16)
     dispatches = {}
-    for b in all_b:
-        for c in range(n_chunks):
-            off, lanes, _, _ = plans[b][c]
-            outgoing = jnp.dot(dispatch[b], scaled[:, off : off + lanes], preferred_element_type=F32)
-            dispatches[b, c] = post(b, c, "d", outgoing)
+    for c in range(n_chunks):
+        off, lanes, _, _ = plans[0][c]
+        outgoing = jnp.dot(dispatch, scaled[:, off : off + lanes], preferred_element_type=F32)
+        for b in all_b:
+            dispatches[b, c] = post(b, c, "d", outgoing[bases[b] : bases[b] + n_exp * batches[b][1]])
 
     for load in w_loads[4:] + down_loads:
         load.start()
@@ -173,15 +176,20 @@
         slot = lane + first
         for e in range(1, n_exp):
             slot = slot + jnp.where(lane >= e * rows, cap - rows, 0)
-        combine[b][...] = jnp.where(slot.astype(F32) == dest_col, 1.0, 0.0).astype(BF16)
+        r["combine"][b][...] = jnp.where(slot.astype(F32) == dest_col, 1.0, 0.0).astype(BF16)
 
     crossing, sides, forwards = {}, {}, {}
+
+    x, acc_g, acc_u, hidden = r["x"], r["acc_g"], r["acc_u"], r["hidden"]
+
+    def rows_of_batch(b):
+        return pl.ds(bases[b], n_exp * batches[b][1])
 
     def gather(b, c):
         off, lanes, _, _ = plans[b][c]
-        x = r["x"][b]
-        x[t, :, off : off + lanes] = collect(b, c, "d", dispatches[b, c])
-        part = x.at[t, :, pl.ds(off, lanes)]
+        here = slice(bases[b], bases[b] + n_exp * batches[b][1])
+        x[t, here, off : off + lanes] = collect(b, c, "d", dispatches[b, c])
+        part = x.at[t, rows_of_batch(b), pl.ds(off, lanes)]
         crossing[b, c] = to_tensor(part, part, "cross", b, c, across)
         sides[b, c] = to_tensor(part, part, "side", b, c, sib)
         crossing[b, c].start()
@@ -190,46 +198,53 @@
     def forward(b, c):
         off, lanes, _, _ = plans[b][c]
         crossing[b, c].wait_recv()
-        part = r["x"][b].at[across, :, pl.ds(off, lanes)]
+        part = x.at[across, rows_of_batch(b), pl.ds(off, lanes)]
         forwards[b, c] = to_tensor(part, part, "fwd", b, c, sib)
         forwards[b, c].start()
 
-    def project(b, c, one, two, begin, end):
-        off, lanes, _, _ = plans[b][c]
-        x, acc_g, acc_u, hidden = r["x"][b], r["acc_g"][b], r["acc_u"][b], r["hidden"][b]
-        feats = slice(off, off + lanes)
+    def project(c, one, two, begin, end, n):
+        off, lanes, _, _ = plans[0][c]
+        feats, cols = slice(off, off + lanes), slice(n, n + tile)
         rows_in = jnp.concatenate([x[one, :, feats], x[two, :, feats]], axis=1)
+
+        def product(w):
+            w_in = jnp.concatenate([w[one, feats, cols], w[two, feats, cols]], axis=0)
+            return jnp.dot(rows_in, w_in, preferred_element_type=F32)
+
+        gate, lift = product(wg), product(wu)
+        if not begin:
+            gate = gate + acc_g[:, cols]
+            lift = lift + acc_u[:, cols]
+        if end:
+            hidden[:, cols] = ((0.5 * gate) * (1.0 + jnp.tanh(0.5 * gate)) * lift).astype(BF16)
+        else:
+            acc_g[:, cols] = gate
+            acc_u[:, cols] = lift
+
+    def near_pair(c, between=()):
+        for b in all_b:
+            sides[b, c].wait_recv()
+        between = list(between)
         for n in range(0, n_ff, tile):
-            cols = slice(n, n + tile)
-
-            def product(w):
-                w_in = jnp.concatenate([w[one, feats, cols], w[two, feats, cols]], axis=0)
-                return jnp.dot(rows_in, w_in, preferred_element_type=F32)
-
-            gate, lift = product(wg), product(wu)
-            if not begin:
-                gate = gate + acc_g[:, cols]
-                lift = lift + acc_u[:, cols]
-            if end:
-                hidden[:, cols] = ((0.5 * gate) * (1.0 + jnp.tanh(0.5 * gate)) * lift).astype(BF16)
-            else:
-                acc_g[:, cols] = gate
-                acc_u[:, cols] = lift
-
-    def near_pair(b, c):
-        sides[b, c].wait_recv()
-        project(b, c, t, sib, c == 0, False)
-
-    def far_pair(b, c):
-        forwards[b, c].wait_recv()
-        project(b, c, across, diag, False, c == n_chunks - 1)
+            project(c, t, sib, c == 0, False, n)
+            if between:
+                step, at_b, at_c = between.pop(0)
+                step(at_b, at_c)
+        for step, at_b, at_c in between:
+            step(at_b, at_c)
+
+    def far_pair(c):
+        for b in all_b:
+            forwards[b, c].wait_recv()
+        for n in range(0, n_ff, tile):
+            project(c, across, diag, False, c == n_chunks - 1, n)
 
     back = list(range(n_chunks))[::-1]
     fars, halves, nears, returns = {}, {}, {}, {}
 
-    def partials(b, one, two, c):
-        off, lanes, _, _ = plans[b][c]
-        rows_in, part = r["hidden"][b][...], slice(off, off + lanes)
+    def partials(one, two, c):
+        off, lanes, _, _ = plans[0][c]
+        rows_in, part = hidden[...], slice(off, off + lanes)
         if lanes % 256:
             both = jnp.dot(
                 rows_in,
@@ -241,83 +256,93 @@
             functools.partial(jnp.dot, rows_in, wd[s, :, part], preferred_element_type=F32) for s in (one, two)
         )
 
-    def start_far(b, c):
-        off, lanes, _, _ = plans[b][c]
+    def start_far(c):
+        off, lanes, _, _ = plans[0][c]
         part = pl.ds(off, lanes)
-        theirs, mine = partials(b, diag, across, c)
-        r["far_out"][b][:, off : off + lanes] = theirs()
-        fars[b, c] = to_tensor(r["far_out"][b].at[:, part], r["far_in"][b].at[:, part], "far", b, c, sib)
-        fars[b, c].start()
-        r["far_own"][b][:, off : off + lanes] = mine()
-
-    def start_half(b, c):
-        off, lanes, _, _ = plans[b][c]
+        theirs, mine = partials(diag, across, c)
+        r["far_out"][:, off : off + lanes] = theirs()
+        fars[c] = to_tensor(r["far_out"].at[:, part], r["far_in"].at[:, part], "far", 0, c, sib)
+        fars[c].start()
+        r["far_own"][:, off : off + lanes] = mine()
+
+    def start_half(c):
+        off, lanes, _, _ = plans[0][c]
         part, lane = pl.ds(off, lanes), slice(off, off + lanes)
-        fars[b, c].wait_recv()
-        r["half_out"][b][:, lane] = (r["far_own"][b][:, lane] + r["far_in"][b][:, lane]).astype(BF16)
-        halves[b, c] = to_tensor(r["half_out"][b].at[:, part], r["half_in"][b].at[:, part], "half", b, c, across)
-        halves[b, c].start()
-
-    def far_side(b):
-        start_far(b, back[0])
+        fars[c].wait_recv()
+        for b in all_b:
+            here = slice(bases[b], bases[b] + n_exp * batches[b][1])
+            r["half_out"][here, lane] = (r["far_own"][here, lane] + r["far_in"][here, lane]).astype(BF16)
+            halves[b, c] = to_tensor(
+                r["half_out"].at[rows_of_batch(b), part], r["half_in"].at[rows_of_batch(b), part], "half", b, c, across
+            )
+            halves[b, c].start()
+
+    def far_side():
+        start_far(back[0])
         for i, c in enumerate(back):
             if i + 1 < n_chunks:
-                start_far(b, back[i + 1])
-            start_half(b, c)
-
-    def near_side(b):
+                start_far(back[i + 1])
+            start_half(c)
+
+    def near_side():
         for c in back:
-            off, lanes, _, _ = plans[b][c]
+            off, lanes, _, _ = plans[0][c]
             part = pl.ds(off, lanes)
-            theirs, mine = partials(b, sib, t, c)
-            r["near_out"][b][:, off : off + lanes] = theirs()
-            nears[b, c] = to_tensor(r["near_out"][b].at[:, part], r["near_in"][b].at[:, part], "near", b, c, sib)
-            nears[b, c].start()
-            r["near_own"][b][:, off : off + lanes] = mine()
-
-    def give_back(b, c):
-        off, lanes, _, _ = plans[b][c]
+            theirs, mine = partials(sib, t, c)
+            r["near_out"][:, off : off + lanes] = theirs()
+            nears[c] = to_tensor(r["near_out"].at[:, part], r["near_in"].at[:, part], "near", 0, c, sib)
+            nears[c].start()
+            r["near_own"][:, off : off + lanes] = mine()
+
+    def give_back(c):
+        off, lanes, _, _ = plans[0][c]
         lane = slice(off, off + lanes)
-        nears[b, c].wait_recv()
-        halves[b, c].wait_recv()
-        total = (
-            r["near_own"][b][:, lane] + r["near_in"][b][:, lane] + r["half_in"][b][:, lane].astype(F32)
-        )
-        returns[b, c] = post(b, c, "r", total)
+        nears[c].wait_recv()
+        for b in all_b:
+            here = slice(bases[b], bases[b] + n_exp * batches[b][1])
+            halves[b, c].wait_recv()
+            total = r["near_own"][here, lane] + r["near_in"][here, lane] + r["half_in"][here, lane].astype(F32)
+            returns[b, c] = post(b, c, "r", total)
 
     last = n_chunks - 1
 
-    gather(0, 0)
+    for b in all_b:
+        gather(b, 0)
     for load in w_loads[:4]:
         load.wait()
-    near_pair(0, 0)
-    for c in range(1, n_chunks):
-        gather(0, c)
-        if c == 1:
-            forward(0, 0)
-        if c < last:
-            near_pair(0, c)
+    meanwhile = []
+    for b in all_b:
+        meanwhile += [(forward, b, 0), (gather, b, 1)]
+    near_pair(0, meanwhile[1:2])
+    for step, b, c in meanwhile[:1] + meanwhile[2:]:
+        step(b, c)
     for load in w_loads[4:]:
         load.wait()
-    far_pair(0, 0)
-    for c in range(1, last):
-        forward(0, c)
-    near_pair(0, last)
-    forward(0, last)
+    far_pair(0)
     for c in range(1, n_chunks):
-        far_pair(0, c)
+        if c < last:
+            for b in all_b:
+                gather(b, c + 1)
+        steps = [(forward, b, c) for b in all_b]
+        if c < last:
+            forward(0, c)
+            steps = steps[1:]
+        near_pair(c, steps)
+        if c > 1:
+            far_pair(c - 1)
+    far_pair(last)
     for load in down_loads:
         load.wait()
-    far_side(0)
-    near_side(0)
+    far_side()
+    near_side()
     for c in back:
-        give_back(0, c)
+        give_back(c)
 
     for c in back:
         off, lanes, _, _ = plans[0][c]
         mixed = None
         for b in all_b:
-            term = jnp.dot(combine[b][...], collect(b, c, "r", returns[b, c]), preferred_element_type=F32)
+            term = jnp.dot(r["combine"][b][...], collect(b, c, "r", returns[b, c]), preferred_element_type=F32)
             mixed = term if mixed is None else mixed + term
         out[:, off : off + lanes] = mixed.astype(BF16)
 
@@ -370,16 +395,13 @@
     lists = {}
     for name in ("send_d", "recv_d", "send_r", "recv_r"):
         lists[name] = [vmem((n_exp, block, 128), BF16) for _, block in made]
-    counts = [n_exp * rows for _, rows in batches]
-    lists["x"] = [vmem((n_ten, n, width), BF16) for n in counts]
-    for name in ("acc_g", "acc_u"):
-        lists[name] = [vmem((n, n_ff), F32) for n in counts]
-    lists["hidden"] = [vmem((n, n_ff), BF16) for n in counts]
-    lists["combine"] = [vmem((tok, n), BF16) for n in counts]
+    lists["combine"] = [vmem((tok, n_exp * rows), BF16) for _, rows in batches]
+    scratch["x"] = vmem((n_ten, slots, width), BF16)
+    scratch["acc_g"] = scratch["acc_u"] = vmem((slots, n_ff), F32)
+    scratch["hidden"] = vmem((slots, n_ff), BF16)
     for name in ("far_out", "far_in", "far_own", "near_out", "near_in", "near_own"):
-        lists[name] = [vmem((n, width), F32) for n in counts]
-    for name in ("half_out", "half_in"):
-        lists[name] = [vmem((n, width), BF16) for n in counts]
+        scratch[name] = vmem((slots, width), F32)
+    scratch["half_out"] = scratch["half_in"] = vmem((slots, width), BF16)
     single = ["tokens_in", "logit_in", "ids_in", "w_gate", "w_up", "w_down", "out"] + list(scratch)
     return pl.pallas_call(
         functools.partial(grouped, n_b, single, list(lists), n_exp, n_ten, cap, batches, plans),

time: 49.1 us -> 47 us (0.957)
  Pallas kernels: 47.1 us -> 45.1 us
    pallas_call x1, Pallas kernels: 47.1 us -> 45.1 us  [fused(): pl.pallas_call(functools.partial(grouped, n_b, single, list(lists), n_exp...]
where the time goes in v6:
time: 47 us; the launch traced here: 46.9 us
  Pallas kernels  45.1 us (96%)
  local copies, waits for them, and re-layouts  1.73 us (4%)
    pallas_call x1, Pallas kernels, fused(): pl.pallas_call(functools.partial(grouped, n_b, single, list(lists), n_exp...  45.1 us
    unnamed x1, local copies, waits for them, and re-layouts  1.73 us

profile of v6, /device:TPU:0, one launch (start us, length us, event | category | flops | bytes accessed | tf_op | source)
XLA Modules:
  0.0 46.9 jit_solution(3937271581254881319)
XLA Ops:
  0.0 45.1 %shard_map.64 = bf16[256,640]{1,0:T(8,128)(2,1)} custom-call(bf16[256,640]{1,0:T(8,128)(2,1)} %refs_0_.1, f32[1,256]{1,0:T(1,128)} %bitcast.2, s32[1,256]{1,0:T(1,128)} %bitcast.3, bf16[1,2560,1024]{2,1,0:T(8,128)(2,1)} %refs_3_.1, bf16[1,2560,1024]{2,1,0:T(8,128)(2,1)} %refs_4_.1, bf16[1,1024,2560]{2,1,0:T(8,128)(2,1)} %refs_5_.1), custom_call_target="tpu_custom_call" | custom-call | flops 5033164800 | bytes 15728640 | tf_op jit(solution)/shard_map/pallas_call | solution.py:406
  45.1 1.7 %copy.8 = bf16[256,640]{1,0:T(8,128)(2,1)} copy(bf16[256,640]{1,0:T(8,128)(2,1)} %shard_map.64) | data formatting | bytes 655360

commit v7 on v4

--- a/solution.py
+++ b/solution.py
@@ -110,8 +110,8 @@
                 pltpu.make_async_remote_copy(
                     src_ref=src.at[e, pl.ds(row, rows)],
                     dst_ref=dst.at[g, pl.ds(row, rows)],
-                    send_sem=r["s_" + kind].at[b, k, c],
-                    recv_sem=r["r_" + kind].at[b, k, c],
+                    send_sem=r["s_" + kind].at[b, c],
+                    recv_sem=r["r_" + kind].at[b, c],
                     device_id=(e, t),
                     device_id_type=MESH,
                 )
@@ -140,29 +140,30 @@
         for copy in copies:
             copy.start()
         dst[g, row : row + rows] = src[g, row : row + rows]
-        sends.extend(copies)
         return copies
 
-    def collect(b, c, kind, copies):
+    def wait_blocks(b, c, kind, side):
+        _, _, row, rows = plans[b][c]
+        part = r[("send_" if side == "s" else "recv_") + kind][b].at[pl.ds(0, n_exp - 1), pl.ds(row, rows)]
+        pltpu.make_async_copy(part, part, r[side + "_" + kind].at[b, c]).wait()
+
+    def collect(b, c, kind):
         _, lanes, row, rows = plans[b][c]
-        for copy in copies:
-            copy.wait_recv()
+        wait_blocks(b, c, kind, "r")
         src = r["recv_" + kind][b]
         return jnp.concatenate(
             [unpack(src[e, row : row + rows], lanes, batches[b][1]) for e in range(n_exp)], axis=0
         ).astype(BF16)
 
-    sends = []
     small[2].wait()
     for load in w_loads[:4]:
         load.start()
     scaled = (factor * tokens[...].astype(F32)).astype(BF16)
-    dispatches = {}
     for b in all_b:
         for c in range(n_chunks):
             off, lanes, _, _ = plans[b][c]
             outgoing = jnp.dot(dispatch[b], scaled[:, off : off + lanes], preferred_element_type=F32)
-            dispatches[b, c] = post(b, c, "d", outgoing)
+            post(b, c, "d", outgoing)
 
     for load in w_loads[4:] + down_loads:
         load.start()
@@ -180,7 +181,7 @@
     def gather(b, c):
         off, lanes, _, _ = plans[b][c]
         x = r["x"][b]
-        x[t, :, off : off + lanes] = collect(b, c, "d", dispatches[b, c])
+        x[t, :, off : off + lanes] = collect(b, c, "d")
         part = x.at[t, :, pl.ds(off, lanes)]
         crossing[b, c] = to_tensor(part, part, "cross", b, c, across)
         sides[b, c] = to_tensor(part, part, "side", b, c, sib)
@@ -225,7 +226,7 @@
         project(b, c, across, diag, False, c == n_chunks - 1)
 
     back = list(range(n_chunks))[::-1]
-    fars, halves, nears, returns = {}, {}, {}, {}
+    fars, halves, nears = {}, {}, {}
 
     def partials(b, one, two, c):
         off, lanes, _, _ = plans[b][c]
@@ -283,7 +284,7 @@
         total = (
             r["near_own"][b][:, lane] + r["near_in"][b][:, lane] + r["half_in"][b][:, lane].astype(F32)
         )
-        returns[b, c] = post(b, c, "r", total)
+        post(b, c, "r", total)
 
     last = n_chunks - 1
 
@@ -310,21 +311,27 @@
         load.wait()
     far_side(0)
     near_side(0)
+    for c in range(n_chunks):
+        wait_blocks(0, c, "d", "s")
+    for group in (crossing, sides, forwards, fars):
+        for copy in group.values():
+            copy.wait_send()
     for c in back:
         give_back(0, c)
+    for group in (halves, nears):
+        for copy in group.values():
+            copy.wait_send()
 
     for c in back:
         off, lanes, _, _ = plans[0][c]
         mixed = None
         for b in all_b:
-            term = jnp.dot(combine[b][...], collect(b, c, "r", returns[b, c]), preferred_element_type=F32)
+            term = jnp.dot(combine[b][...], collect(b, c, "r"), preferred_element_type=F32)
             mixed = term if mixed is None else mixed + term
         out[:, off : off + lanes] = mixed.astype(BF16)
 
-    for group in (crossing, sides, forwards, fars, halves, nears):
-        sends.extend(group.values())
-    for copy in sends:
-        copy.wait_send()
+    for c in back:
+        wait_blocks(0, c, "r", "s")
 
 
 def grouped(n_b, single, per_batch, n_exp, n_ten, cap, batches, plans, *refs):
@@ -362,8 +369,8 @@
         "w_sem": dma((3, n_ten)),
     }
     for kind in ("d", "r"):
-        scratch["s_" + kind] = dma((n_b, n_exp, n_c))
-        scratch["r_" + kind] = dma((n_b, n_exp, n_c))
+        scratch["s_" + kind] = dma((n_b, n_c))
+        scratch["r_" + kind] = dma((n_b, n_c))
     for kind in ("cross", "side", "fwd", "far", "half", "near"):
         scratch["s_" + kind] = dma((n_b, n_c))
         scratch["r_" + kind] = dma((n_b, n_c))

time: 45.5 us -> 44.8 us (0.985)
  Pallas kernels: 43.6 us -> 42.9 us
    pallas_call x1, Pallas kernels: 43.6 us -> 42.9 us  [fused(): pl.pallas_call(functools.partial(grouped, n_b, single, list(lists), n_exp...]
where the time goes in v7:
time: 44.8 us; the launch traced here: 44.6 us
  Pallas kernels  42.9 us (96%)
  local copies, waits for them, and re-layouts  1.73 us (4%)
    pallas_call x1, Pallas kernels, fused(): pl.pallas_call(functools.partial(grouped, n_b, single, list(lists), n_exp...  42.9 us
    unnamed x1, local copies, waits for them, and re-layouts  1.73 us

profile of v7, /device:TPU:0, one launch (start us, length us, event | category | flops | bytes accessed | tf_op | source)
XLA Modules:
  0.0 44.6 jit_solution(16814918084070570454)
XLA Ops:
  0.0 42.9 %shard_map.64 = bf16[256,640]{1,0:T(8,128)(2,1)} custom-call(bf16[256,640]{1,0:T(8,128)(2,1)} %refs_0_.1, f32[1,256]{1,0:T(1,128)} %bitcast.2, s32[1,256]{1,0:T(1,128)} %bitcast.3, bf16[1,2560,1024]{2,1,0:T(8,128)(2,1)} %refs_3_.1, bf16[1,2560,1024]{2,1,0:T(8,128)(2,1)} %refs_4_.1, bf16[1,1024,2560]{2,1,0:T(8,128)(2,1)} %refs_5_.1), custom_call_target="tpu_custom_call" | custom-call | flops 5033164800 | bytes 15728640 | tf_op jit(solution)/shard_map/pallas_call | solution.py:391
  42.9 1.7 %copy.8 = bf16[256,640]{1,0:T(8,128)(2,1)} copy(bf16[256,640]{1,0:T(8,128)(2,1)} %shard_map.64) | data formatting | bytes 655360
